TPU v7x, 32 devices: a whole 2x2x4 slice. The times are simulated.
32 devices in a mesh: ctx: 8 (over z, x), head: 4 (over y, core).
Axes of the slice: x: 2, y: 2, z: 4, core: 2. Of those that a mesh axis runs over, the one named last changes fastest.
Arguments:
- x_raw: bfloat16 [2048, 8192], P('ctx', 'head'), may hold values from -6 to 6
- bc_raw: bfloat16 [2048, 256], P('ctx'), may hold values from -6 to 6
- conv_x_w: bfloat16 [4, 8192], P(None, 'head'), may hold values from -3 to 3
- conv_bc_w: bfloat16 [4, 256], replicated, may hold values from -3 to 3
- dt_raw: float32 [128, 2048], P('head', 'ctx'), may hold values from -7 to 0
- a_log: float32 [128], P('head'), may hold values from -10 to 1
- d_skip: float32 [128], P('head'), may hold values from 0.5 to 1.5
- doc_starts: int32 [8], P('ctx'), may hold values from 0 to 256, as said below
- grad_y: bfloat16 [2048, 8192], P('ctx', 'head'), may hold values from -6 to 6
Outputs:
- y_out: bfloat16 [2048, 8192], P('ctx', 'head')
- grad_x_raw: bfloat16 [2048, 8192], P('ctx', 'head')
- grad_bc_raw: bfloat16 [2048, 256], P('ctx')
- grad_dt_raw: float32 [128, 2048], P('head', 'ctx')
Inputs may be any that keep to these rules, and one draw needn't show every extreme that they name: Block b holds a document start at row 256 * b + doc_starts[b] when doc_starts[b] < 256, and none when doc_starts[b] = 256; doc_starts[0] = 0.
All inputs are finite; a program needn't handle non-finite values.
Results may differ from a plain program's by a relative error of at most 0.013.
Values may be sent and summed in bfloat16 or wider, within the bound.
A program may use at most 128 MiB of HBM per device.

v0:
```python
import jax
import jax.numpy as jnp
from jax import lax
from jax.sharding import PartitionSpec as P


def shifted(x, axis, by):
    size = lax.axis_size(axis)
    pairs = [(i, i + by) for i in range(size) if 0 <= i + by < size]
    return lax.ppermute(x, axis, pairs)


def entering_2(value, axis, join, neutral, backward):
    count, mine = (lax.axis_size(axis), lax.axis_index(axis))
    pieces = jax.tree.map(lambda part: lax.all_gather(part, axis), value)
    if backward:
        pieces = jax.tree.map(lambda part: part[::-1], pieces)
        mine = count - 1 - mine
    so_far = jax.tree.map(
        lambda part, zero: jnp.full_like(part, 0) + jnp.asarray(zero, part.dtype), value, neutral
    )

    def step(position, so_far):
        longer = join(so_far, jax.tree.map(lambda part: part[position], pieces))
        return jax.tree.map(lambda new, old: jnp.where(position < mine, new, old), longer, so_far)

    return lax.fori_loop(0, count - 1, step, so_far)


def contract(pattern, first_op, second_op):
    return jnp.einsum(pattern, first_op, second_op, preferred_element_type=jnp.float32)


def contract_exact(pattern, first_op, second_op):
    return jnp.einsum(
        pattern,
        first_op.astype(jnp.float32),
        second_op.astype(jnp.float32),
        precision=lax.Precision.HIGHEST,
    )


def silu_grad(values):
    sigmoid_v = jax.nn.sigmoid(values)
    return sigmoid_v * (1.0 + values * (1.0 - sigmoid_v))


def causal_conv(tok_rows, before, weight):
    row_count = tok_rows.shape[0]
    tap_count = weight.shape[0]
    padded = jnp.concatenate([before, tok_rows], axis=0).astype(jnp.float32)
    weight_f = weight.astype(jnp.float32)
    running = jnp.zeros(tok_rows.shape, jnp.float32)
    for offset in range(tap_count):
        running = running + weight_f[offset] * padded[offset : offset + row_count]
    return running


def conv_back(gradient, following, weight):
    row_count = gradient.shape[0]
    tap_count = weight.shape[0]
    padded = jnp.concatenate([gradient, following], axis=0)
    weight_f = weight.astype(jnp.float32)
    running = jnp.zeros(gradient.shape, jnp.float32)
    for offset in range(tap_count):
        running = running + weight_f[tap_count - 1 - offset] * padded[offset : offset + row_count]
    return running


def block_prep(x_block, bc_block, step_block, decay_rate, reset_at):
    block_len = step_block.shape[1]
    nstate = bc_block.shape[1] // 2
    position = jnp.arange(block_len, dtype=jnp.int32)
    segment = position >= reset_at
    cumulated = jnp.cumsum(-decay_rate[:, None] * step_block, axis=1)
    causal = (segment[:, None] == segment[None, :]) & (position[:, None] >= position[None, :])
    kernel = jnp.exp(
        jnp.where(causal[None], cumulated[:, :, None] - cumulated[:, None, :], -jnp.inf)
    )
    entering = jnp.where(segment[None, :], 0.0, jnp.exp(cumulated))
    final_cum = cumulated[:, block_len - 1 :]
    leaving = jnp.where(
        segment[None, :] == segment[block_len - 1], jnp.exp(final_cum - cumulated), 0.0
    )
    carry_out = jnp.where(reset_at >= block_len, jnp.exp(cumulated[:, block_len - 1]), 0.0)
    b_matrix = bc_block[:, :nstate]
    c_matrix = bc_block[:, nstate:]
    gram_mat = contract("tn,sn->ts", c_matrix, b_matrix)
    mixing = (gram_mat[None] * kernel).astype(jnp.bfloat16)
    x_float = x_block.astype(jnp.float32)
    scaled_x = (x_float * jnp.transpose(step_block)[:, :, None]).astype(jnp.bfloat16)
    leaving_x = (x_float * jnp.transpose(leaving * step_block)[:, :, None]).astype(jnp.bfloat16)
    return dict(
        kernel=kernel,
        entering=entering,
        leaving=leaving,
        carry_out=carry_out,
        b_matrix=b_matrix,
        c_matrix=c_matrix,
        gram_mat=gram_mat,
        mixing=mixing,
        scaled_x=scaled_x,
        leaving_x=leaving_x,
    )


def block_state(prepared):
    return contract("shp,sn->hpn", prepared["leaving_x"], prepared["b_matrix"])


def block_out(prepared, x_block, d_skip, state_in):
    state_q = state_in.astype(jnp.bfloat16)
    intra = contract("hts,shp->thp", prepared["mixing"], prepared["scaled_x"])
    y_state = contract("tn,hpn->thp", prepared["c_matrix"], state_q)
    result = (
        intra
        + jnp.transpose(prepared["entering"])[:, :, None] * y_state
        + d_skip[None, :, None] * x_block.astype(jnp.float32)
    )
    return (result.astype(jnp.bfloat16), y_state)


def block_bsum(prepared, output_grad_block):
    enter_dy = (
        output_grad_block.astype(jnp.float32) * jnp.transpose(prepared["entering"])[:, :, None]
    ).astype(jnp.bfloat16)
    return (enter_dy, contract("thp,tn->hpn", enter_dy, prepared["c_matrix"]))


def block_back(
    prepared,
    x_block,
    output_grad_block,
    enter_dy,
    y_state,
    state_in,
    dstate,
    decay_rate,
    d_skip,
    step_block,
):
    block_len = step_block.shape[1]
    kernel = prepared["kernel"]
    dstate_q = dstate.astype(jnp.bfloat16)
    state_q = state_in.astype(jnp.bfloat16)
    response = contract("thp,shp->hts", output_grad_block, prepared["scaled_x"])
    weighed = response * kernel
    z_term = weighed * prepared["gram_mat"][None]
    d_gram = jnp.sum(weighed, axis=0)
    grad_c = contract_exact("ts,sn->tn", d_gram, prepared["b_matrix"]) + contract(
        "thp,hpn->tn", enter_dy, state_q
    )
    grad_b = contract_exact("ts,tn->sn", d_gram, prepared["c_matrix"]) + contract(
        "shp,hpn->sn", prepared["leaving_x"], dstate_q
    )
    d_scaled = contract("hts,thp->shp", prepared["mixing"], output_grad_block)
    d_leaving = contract("sn,hpn->shp", prepared["b_matrix"], dstate_q)
    x_float = x_block.astype(jnp.float32)
    step_t = jnp.transpose(step_block)
    leave_t = jnp.transpose(prepared["leaving"])
    grad_xc = (
        step_t[:, :, None] * d_scaled
        + (leave_t * step_t)[:, :, None] * d_leaving
        + d_skip[None, :, None] * output_grad_block.astype(jnp.float32)
    )
    along_dt = jnp.transpose(jnp.sum(x_float * d_scaled, axis=2))
    along_leave = jnp.transpose(jnp.sum(x_float * d_leaving, axis=2))
    leave_term = prepared["leaving"] * step_block * along_leave
    enter_term = prepared["entering"] * jnp.transpose(
        jnp.sum(output_grad_block.astype(jnp.float32) * y_state, axis=2)
    )
    final_term = jnp.sum(leave_term, axis=1) + prepared["carry_out"] * jnp.sum(
        dstate * state_in, axis=(1, 2)
    )
    is_final = jnp.arange(block_len, dtype=jnp.int32) == block_len - 1
    d_cum = jnp.sum(z_term, axis=2) - jnp.sum(z_term, axis=1) + enter_term - leave_term
    d_cum = d_cum + jnp.where(is_final[None, :], final_term[:, None], 0.0)
    d_log = lax.cumsum(d_cum, axis=1, reverse=True)
    grad_step = along_dt + prepared["leaving"] * along_leave - decay_rate[:, None] * d_log
    return (grad_b, grad_c, grad_xc, grad_step)


def compose(earlier, later):
    return (earlier[0] * later[0], later[0][:, None, None] * earlier[1] + later[1])


def body(x_raw, bc_raw, conv_x_w, conv_bc_w, dt_raw, a_log, d_skip, doc_starts, grad_y):
    tok_rows, channels = x_raw.shape
    head_count = a_log.shape[0]
    head_dim = channels // head_count
    nstate = bc_raw.shape[1] // 2
    rim_rows = conv_x_w.shape[0] - 1
    nblock = doc_starts.shape[0]
    block_len = tok_rows // nblock
    prev_x, prev_bc = shifted(
        (x_raw[tok_rows - rim_rows :], bc_raw[tok_rows - rim_rows :]), "ctx", 1
    )
    x_pre = causal_conv(x_raw, prev_x, conv_x_w)
    bc_pre = causal_conv(bc_raw, prev_bc, conv_bc_w)
    x_conv = jax.nn.silu(x_pre).astype(jnp.bfloat16)
    bc_conv = jax.nn.silu(bc_pre).astype(jnp.bfloat16)
    step_size = jax.nn.softplus(dt_raw)
    decay_rate = jnp.exp(a_log)
    block_id = 0
    x_block = x_conv.reshape(block_len, head_count, head_dim)
    preps = [block_prep(x_block, bc_conv, step_size, decay_rate, doc_starts[block_id])]
    x_blocks = [x_block]
    step_blocks = [step_size]
    dy_blocks = [grad_y.reshape(block_len, head_count, head_dim)]
    state_shape = (head_count, head_dim, nstate)
    identity = (jnp.ones((head_count,), jnp.float32), jnp.zeros(state_shape, jnp.float32))
    block_sums = [block_state(prepared) for prepared in preps]
    dev_carry = jnp.ones((head_count,), jnp.float32)
    dev_state = jnp.zeros(state_shape, jnp.float32)
    block_id = 0
    dev_state = preps[block_id]["carry_out"][:, None, None] * dev_state + block_sums[block_id]
    dev_carry = dev_carry * preps[block_id]["carry_out"]
    chained = entering_2((dev_carry, dev_state), "ctx", compose, identity, False)
    state_in = chained[1]
    block_id = 0
    states = [state_in]
    y_block, y_state = block_out(preps[block_id], x_blocks[block_id], d_skip, state_in)
    y_parts = y_block.reshape(block_len, channels)
    y_states = [y_state]
    block_id = 0
    enter_dy, back_part = block_bsum(preps[block_id], dy_blocks[block_id])
    enter_list = [enter_dy]
    back_list = [back_part]
    dev_grad = jnp.zeros(state_shape, jnp.float32)
    for block_id in reversed(range(nblock)):
        dev_grad = preps[block_id]["carry_out"][:, None, None] * dev_grad + back_list[block_id]
    chained_back = entering_2((dev_carry, dev_grad), "ctx", compose, identity, True)
    dstate = chained_back[1]
    dstates = [dstate] * nblock
    for block_id in reversed(range(nblock)):
        dstates[block_id] = dstate
        dstate = preps[block_id]["carry_out"][:, None, None] * dstate + back_list[block_id]
    block_id = 0
    grad_b, grad_c, grad_xc, grad_step = block_back(
        preps[block_id],
        x_blocks[block_id],
        dy_blocks[block_id],
        enter_list[block_id],
        y_states[block_id],
        states[block_id],
        dstates[block_id],
        decay_rate,
        d_skip,
        step_blocks[block_id],
    )
    grad_b_list = [grad_b]
    grad_c_list = [grad_c]
    grad_xc_list = grad_xc.reshape(block_len, channels)
    grad_step_list = [grad_step]
    grad_bc = jnp.concatenate(
        [jnp.concatenate(grad_b_list, axis=0), jnp.concatenate(grad_c_list, axis=0)], axis=1
    )
    grad_bc_pre = lax.psum(grad_bc, "head") * silu_grad(bc_pre)
    grad_x_pre = grad_xc_list * silu_grad(x_pre)
    next_x, next_bc = shifted((grad_x_pre[:rim_rows], grad_bc_pre[:rim_rows]), "ctx", -1)
    grad_x_raw = conv_back(grad_x_pre, next_x, conv_x_w).astype(jnp.bfloat16)
    grad_bc_part = conv_back(grad_bc_pre, next_bc, conv_bc_w).astype(jnp.bfloat16)
    grad_dt_raw = jnp.concatenate(grad_step_list, axis=1) * jax.nn.sigmoid(dt_raw)
    return (y_parts, grad_x_raw, grad_bc_part, grad_dt_raw)


def solution(mesh):
    in_specs = (
        P("ctx", "head"),
        P("ctx", None),
        P(None, "head"),
        P(),
        P("head", "ctx"),
        P("head"),
        P("head"),
        P("ctx"),
        P("ctx", "head"),
    )
    out_specs = (P("ctx", "head"), P("ctx", "head"), P("ctx", None), P("head", "ctx"))
    return jax.shard_map(body, mesh=mesh, in_specs=in_specs, out_specs=out_specs, check_vma=False)
```

profile of v0, /device:TPU:0, one launch (start us, length us, event | category | flops | bytes accessed | tf_op | source)
XLA Modules:
  0.0 384.0 jit_solution(12766547721595696778)
XLA Ops:
  7.9 4.8 %collective-permute-start.1 = (bf16[3,256]{1,0:T(4,128)(2,1)S(1)}, bf16[3,256]{1,0:T(4,128)(2,1)S(1)}, u32[]{:S(2)}, u32[]{:S(2)}) collective-permute-start(bf16[3,256]{1,0:T(4,128)(2,1)S(1)} %slice.121), channel_id=1, source_target_pairs={{0,4},{4,8},{8,12},{12,16},{16,20},{20,24},{24,28},{1,5},{5,9},{9,... | collective-permute-start | bytes 4616 | tf_op jit(solution)/shard_map/ppermute | solution.py:10
  20.6 1.5 copy.96
  25.4 4.1 %collective-permute-start = (bf16[3,2048]{1,0:T(4,128)(2,1)S(1)}, bf16[3,2048]{1,0:T(4,128)(2,1)}, u32[]{:S(2)}, u32[]{:S(2)}) collective-permute-start(bf16[3,2048]{1,0:T(4,128)(2,1)S(1)} %slice.112), channel_id=1, source_target_pairs={{0,4},{4,8},{8,12},{12,16},{16,20},{20,24},{24,28},{1,5},{5,9},{9,... | collective-permute-start | bytes 36872 | tf_op jit(solution)/shard_map/ppermute | solution.py:10
  30.1 18.7 %all-reduce = f32[256]{0:T(256)S(1)} all-reduce(f32[256]{0:T(256)S(1)} %get-tuple-element.294), channel_id=2, replica_groups=mesh['ctx'=8,'head'=4] {'ctx'}, use_global_device_ids=true, to_apply=%add | all-reduce | flops 256 | bytes 2048
  52.3 1.5 maximum_convert_fusion
  53.8 96.4 %all-gather.8.cloned.1.call-done = f32[256,64,128]{2,1,0:T(8,128)} async-done(((f32[32,64,128]{2,1,0:T(8,128)}), f32[256,64,128]{2,1,0:T(8,128)}) %all-gather.8.cloned.1.call-update) | async-done | bytes 8388624 | tf_op jit(solution)/shard_map/all_gather | solution.py:15
  150.2 8.3 %rev.7 = f32[8,32,64,128]{3,2,1,0:T(8,128)} reverse(f32[8,32,64,128]{3,2,1,0:T(8,128)} %bitcast.191), dimensions={0} | reverse | bytes 16777216 | tf_op jit(solution)/shard_map/rev | solution.py:17
  158.5 15.1 %while.29 = (s32[]{:T(128)}, f32[32,64,128]{2,1,0:T(8,128)S(1)}, s32[]{:T(128)}, f32[8,32]{1,0:T(8,128)}, f32[8,32,64,128]{3,2,1,0:T(8,128)}, /*index=5*/s32[]{:T(128)}, s32[]{:T(128)}) while((s32[]{:T(128)}, f32[32,64,128]{2,1,0:T(8,128)S(1)}, s32[]{:T(128)}, f32[8,32]{1,0:T(8,128)}, f32[8,32,64,128]{3,2,1,0:T(8,128)}, ...), condition=%wide.region_5.6_spmd.clone, body=%wide.region_4.5_spmd.clone.sunk | while | flops 1048580 | bytes 3146217 | solution.py:27
  159.2 1.5 fusion.100
  161.3 1.5 fusion.100
  163.5 1.5 fusion.100
  165.7 1.5 fusion.100
  167.8 1.5 fusion.100
  170.0 1.5 fusion.100
  174.9 4.1 %fusion.24 = (f32[256,32,64]{0,2,1:T(8,128)}, f32[32,256,64]{1,2,0:T(8,128)}) fusion(f32[256,32,64]{0,2,1:T(8,128)S(1)} %fusion.51, f32[256,32]{0,1:T(8,128)S(1)} %copy-done.34, f32[32]{0:T(128)S(1)} %copy-done.57, f32[256,32]{0,1:T(8,128)S(1)} %copy-done.30, bf16[256,2048]{0,1:T(8,128)(2,1)S(1)} %copy-done.3, bf16[256,32,64]{0,2,1:T(8,128)(2,1)S(1)} %bitcast.188, ...), kind=kOutput, calls=%fused_computation.38 | convolution fusion | flops 279969792 | bytes 8814720 | tf_op jit(solution)/shard_map/hts,thp->shp/dot_general | solution.py:31
  179.0 2.9 copy.98
  181.9 4.5 %multiply_multiply_fusion = (f32[256,2048]{1,0:T(8,128)}, f32[256,2048]{1,0:T(8,128)S(1)}) fusion(f32[256,2048]{1,0:T(8,128)} %copy.98, f32[259,2048]{1,0:T(8,128)S(1)} %maximum_convert_fusion, f32[2048]{0:T(1024)S(1)} %bitcast.202, f32[2048]{0:T(1024)S(1)} %bitcast.200, f32[2048]{0:T(1024)S(1)} %bitcast.198, f32[2048]{0:T(1024)S(1)} %bitcast.196), kind=kLoop, calls=%fused_computation.57 | loop fusion | flops 7864320 | bytes 14712832 | tf_op jit(solution)/shard_map/mul | solution.py:259
  186.4 1.9 fusion.34
  188.3 1.9 copy.90
  190.3 4.4 %fusion.31 = (f32[256,32]{0,1:T(8,128)}, f32[256,32]{0,1:T(8,128)S(1)}) fusion(f32[32,256,64]{1,2,0:T(8,128)} %get-tuple-element.296, f32[256,2048]{0,1:T(8,128)S(1)} %copy.90, f32[256,32,64]{0,2,1:T(8,128)} %copy-done.6), kind=kLoop, calls=%fused_computation.52 | loop fusion | flops 2080768 | bytes 6356992 | tf_op jit(solution)/shard_map/reduce_sum | solution.py:166
  198.0 1.5 collective-permute-start.2
  199.4 2.1 convolution_bitcast_fusion.1
  201.6 5.7 %multiply_reduce_fusion = (f32[32,256]{1,0:T(8,128)}, f32[32,256]{1,0:T(8,128)}, f32[256,256]{0,1:T(8,128)S(1)}) fusion(f32[32,256]{1,0:T(8,128)S(1)} %copy_bitcast_fusion, f32[256,256]{0,1:T(8,128)S(1)} %copy-done.14, pred[256,256]{0,1:T(8,128)(4,1)S(1)} %fusion.56, bf16[256,32,64]{0,2,1:T(8,128)(2,1)S(1)} %bitcast.189, f32[256,32,64]{0,2,1:T(8,128)S(1)} %bitcast.186, ...), kind=kOutput, calls=%fused_computation.9 | convolution fusion | flops 284082176 | bytes 3866624 | tf_op jit(solution)/shard_map/thp,shp->hts/dot_general | solution.py:31
  208.3 1.9 fusion.19
  210.2 110.2 %all-gather.6.cloned.1.call-done = f32[256,64,128]{2,1,0:T(8,128)} async-done(((f32[32,64,128]{2,1,0:T(8,128)}), f32[256,64,128]{2,1,0:T(8,128)}) %all-gather.6.cloned.1.call-update) | async-done | bytes 8388624 | tf_op jit(solution)/shard_map/all_gather | solution.py:15
  320.5 15.1 %while.28 = (s32[]{:T(128)}, f32[32,64,128]{2,1,0:T(8,128)S(1)}, s32[]{:T(128)}, f32[8,32]{1,0:T(8,128)}, f32[8,32,64,128]{3,2,1,0:T(8,128)}, /*index=5*/s32[]{:T(128)}, s32[]{:T(128)}) while((s32[]{:T(128)}, f32[32,64,128]{2,1,0:T(8,128)S(1)}, s32[]{:T(128)}, f32[8,32]{1,0:T(8,128)}, f32[8,32,64,128]{3,2,1,0:T(8,128)}, ...), condition=%wide.region_3.4_spmd.clone, body=%wide.region_2.3_spmd.clone.sunk | while | flops 1048580 | bytes 3146217 | solution.py:27
  321.1 1.5 fusion.99
  335.9 1.8 fusion.25
  339.9 4.6 %fusion.33 = bf16[256,32,64]{0,2,1:T(8,128)(2,1)S(1)} fusion(f32[256,32,64]{0,2,1:T(8,128)} %bitcast.185, f32[256,32,64]{0,2,1:T(8,128)} %get-tuple-element.298, f32[32,256]{1,0:T(8,128)S(1)} %copy-done.23, f32[256,256]{0,1:T(8,128)S(1)} %copy-done.15, pred[256,256]{0,1:T(8,128)(4,1)S(1)} %copy-done.25, f32[32]{0:T(128)S(1)} %copy-done.58, ...), kind=kOutput, calls=%fused_computation.55 | convolution fusion | flops 280494080 | bytes 5668992 | tf_op jit(solution)/shard_map/hts,shp->thp/dot_general | solution.py:31
  344.8 2.5 reduce-window.16
  347.4 22.7 %all-reduce.3.cloned.1.call-done = f32[256,256]{1,0:T(8,128)} async-done(((f32[256,256]{1,0:T(8,128)}), f32[256,256]{1,0:T(8,128)}) %all-reduce.3.cloned.1.call-update) | async-done | bytes 262160 | tf_op jit(solution)/shard_map/psum | solution.py:258
  374.6 2.1 collective-permute-done.3
  (199 shorter events, 47.7 us)
Async XLA Ops:
  7.2 14.9 %copy-start.16 = (bf16[256,256]{1,0:T(8,128)(2,1)S(1)}, bf16[256,256]{1,0:T(8,128)(2,1)}, u32[]{:S(2)}) copy-start(bf16[256,256]{1,0:T(8,128)(2,1)} %param.14) | copy-start | bytes 393220
  7.2 143.0 %all-gather.8.cloned.1.call-start = ((), (), s32[]{:S(2)}) async-start(), calls=%async_computation.2 | async-start | bytes 9437184 | tf_op jit(solution)/shard_map/all_gather | solution.py:15
  7.9 14.2 %collective-permute-start.1 = (bf16[3,256]{1,0:T(4,128)(2,1)S(1)}, bf16[3,256]{1,0:T(4,128)(2,1)S(1)}, u32[]{:S(2)}, u32[]{:S(2)}) collective-permute-start(bf16[3,256]{1,0:T(4,128)(2,1)S(1)} %slice.121), channel_id=1, source_target_pairs={{0,4},{4,8},{8,12},{12,16},{16,20},{20,24},{24,28},{1,5},{5,9},{9,... | collective-permute-start | bytes 4616 | tf_op jit(solution)/shard_map/ppermute | solution.py:10
  16.1 34.1 %copy-start.27 = (f32[32,2]{0,1:T(2,128)}, f32[32,2]{0,1:T(2,128)S(1)}, u32[]{:S(2)}) copy-start(f32[32,2]{0,1:T(2,128)S(1)} %slice.132) | copy-start | bytes 772
  16.2 185.3 %copy-start.22 = (f32[32,256]{1,0:T(8,128)}, f32[32,256]{1,0:T(8,128)S(1)}, u32[]{:S(2)}) copy-start(f32[32,256]{1,0:T(8,128)S(1)} %copy_bitcast_fusion) | copy-start | bytes 98308
  16.4 33.9 %copy-start.35 = (f32[32,1]{0,1:T(1,128)}, f32[32,1]{0,1:T(1,128)S(1)}, u32[]{:S(2)}) copy-start(f32[32,1]{0,1:T(1,128)S(1)} %copy.115) | copy-start | bytes 388
  17.6 32.5 %copy-start.47 = (pred[256]{0:T(512)(128)(4,1)}, pred[256]{0:T(512)(128)(4,1)S(1)}, u32[]{:S(2)}) copy-start(pred[256]{0:T(512)(128)(4,1)S(1)} %get-tuple-element.300) | copy-start | bytes 772
  17.7 6.9 %copy-start.11 = (f32[256,32]{0,1:T(8,128)}, f32[256,32]{0,1:T(8,128)S(1)}, u32[]{:S(2)}) copy-start(f32[256,32]{0,1:T(8,128)S(1)} %fusion.77) | copy-start | bytes 98308
  18.5 6.0 %copy-start.39 = (f32[1,256]{1,0:T(1,128)}, f32[1,256]{1,0:T(1,128)S(1)}, u32[]{:S(2)}) copy-start(f32[1,256]{1,0:T(1,128)S(1)} %get-tuple-element.287) | copy-start | bytes 3076
  18.5 6.0 %copy-start.41 = (f32[1,256]{1,0:T(1,128)}, f32[1,256]{1,0:T(1,128)S(1)}, u32[]{:S(2)}) copy-start(f32[1,256]{1,0:T(1,128)S(1)} %get-tuple-element.288) | copy-start | bytes 3076
  18.5 6.0 %copy-start.43 = (f32[1,256]{1,0:T(1,128)}, f32[1,256]{1,0:T(1,128)S(1)}, u32[]{:S(2)}) copy-start(f32[1,256]{1,0:T(1,128)S(1)} %get-tuple-element.289) | copy-start | bytes 3076
  18.6 6.0 %copy-start.45 = (f32[1,256]{1,0:T(1,128)}, f32[1,256]{1,0:T(1,128)S(1)}, u32[]{:S(2)}) copy-start(f32[1,256]{1,0:T(1,128)S(1)} %get-tuple-element.290) | copy-start | bytes 3076
  22.2 28.5 %copy-start.10 = (f32[32,256]{1,0:T(8,128)S(1)}, f32[32,256]{1,0:T(8,128)}, u32[]{:S(2)}) copy-start(f32[32,256]{1,0:T(8,128)} %param.17) | copy-start | bytes 98308
  23.1 28.2 %copy-start.26 = (bf16[4,2048]{1,0:T(4,128)(2,1)S(1)}, bf16[4,2048]{1,0:T(4,128)(2,1)}, u32[]{:S(2)}) copy-start(bf16[4,2048]{1,0:T(4,128)(2,1)} %param.15) | copy-start | bytes 49156
  24.6 295.9 %all-gather.6.cloned.1.call-start = ((), (), s32[]{:S(2)}) async-start(), calls=%async_computation.1 | async-start | bytes 9437184 | tf_op jit(solution)/shard_map/all_gather | solution.py:15
  25.4 26.8 %collective-permute-start = (bf16[3,2048]{1,0:T(4,128)(2,1)S(1)}, bf16[3,2048]{1,0:T(4,128)(2,1)}, u32[]{:S(2)}, u32[]{:S(2)}) collective-permute-start(bf16[3,2048]{1,0:T(4,128)(2,1)S(1)} %slice.112), channel_id=1, source_target_pairs={{0,4},{4,8},{8,12},{12,16},{16,20},{20,24},{24,28},{1,5},{5,9},{9,... | collective-permute-start | bytes 36872 | tf_op jit(solution)/shard_map/ppermute | solution.py:10
  50.2 151.3 %copy-start.24 = (pred[256,256]{0,1:T(8,128)(4,1)}, pred[256,256]{0,1:T(8,128)(4,1)S(1)}, u32[]{:S(2)}) copy-start(pred[256,256]{0,1:T(8,128)(4,1)S(1)} %fusion.56) | copy-start | bytes 196612
  51.4 130.5 %copy-start.18 = (f32[1,2048]{1,0:T(1,128)}, f32[1,2048]{1,0:T(1,128)S(1)}, u32[]{:S(2)}) copy-start(f32[1,2048]{1,0:T(1,128)S(1)} %get-tuple-element.285) | copy-start | bytes 24580
  51.4 130.5 %copy-start.20 = (f32[1,2048]{1,0:T(1,128)}, f32[1,2048]{1,0:T(1,128)S(1)}, u32[]{:S(2)}) copy-start(f32[1,2048]{1,0:T(1,128)S(1)} %get-tuple-element.286) | copy-start | bytes 24580
  196.9 173.2 %all-reduce.3.cloned.1.call-start = ((), (), s32[]{:S(2)}) async-start(), calls=%async_computation | async-start | bytes 524288 | tf_op jit(solution)/shard_map/psum | solution.py:258
  198.0 10.3 %collective-permute-start.2 = (f32[3,2048]{1,0:T(4,128)S(1)}, f32[3,2048]{1,0:T(4,128)S(1)}, u32[]{:S(2)}, u32[]{:S(2)}) collective-permute-start(f32[3,2048]{1,0:T(4,128)S(1)} %slice.165), channel_id=1, source_target_pairs={{4,0},{8,4},{12,8},{16,12},{20,16},{24,20},{28,24},{5,1},{9,5},{13... | collective-permute-start | bytes 73736 | tf_op jit(solution)/shard_map/ppermute | solution.py:10
  201.6 6.7 %copy-start.5 = (f32[256,2048]{1,0:T(8,128)S(1)}, f32[256,2048]{1,0:T(8,128)}, u32[]{:S(2)}) copy-start(f32[256,2048]{1,0:T(8,128)} %get-tuple-element.275) | copy-start | bytes 6291460
  201.6 6.7 %copy-start.19 = (f32[1,2048]{1,0:T(1,128)S(1)}, f32[1,2048]{1,0:T(1,128)}, u32[]{:S(2)}) copy-start(f32[1,2048]{1,0:T(1,128)} %copy-done.18) | copy-start | bytes 24580
  201.6 6.7 %copy-start.21 = (f32[1,2048]{1,0:T(1,128)S(1)}, f32[1,2048]{1,0:T(1,128)}, u32[]{:S(2)}) copy-start(f32[1,2048]{1,0:T(1,128)} %copy-done.20) | copy-start | bytes 24580
  339.9 30.2 %copy-start.7 = (f32[256,256]{1,0:T(8,128)S(1)}, f32[256,256]{1,0:T(8,128)}, u32[]{:S(2)}) copy-start(f32[256,256]{1,0:T(8,128)} %get-tuple-element.278) | copy-start | bytes 786436
  339.9 32.6 %copy-start.17 = (f32[256,32]{0,1:T(8,128)S(1)}, f32[256,32]{0,1:T(8,128)}, u32[]{:S(2)}) copy-start(f32[256,32]{0,1:T(8,128)} %get-tuple-element.253) | copy-start | bytes 98308
  339.9 32.6 %copy-start.55 = (f32[32]{0:T(128)S(1)}, f32[32]{0:T(128)}, u32[]{:S(2)}) copy-start(f32[32]{0:T(128)} %get-tuple-element.291) | copy-start | bytes 388
  344.5 32.1 %copy-start.40 = (f32[1,256]{1,0:T(1,128)S(1)}, f32[1,256]{1,0:T(1,128)}, u32[]{:S(2)}) copy-start(f32[1,256]{1,0:T(1,128)} %copy-done.39) | copy-start | bytes 3076
  344.5 32.1 %copy-start.42 = (f32[1,256]{1,0:T(1,128)S(1)}, f32[1,256]{1,0:T(1,128)}, u32[]{:S(2)}) copy-start(f32[1,256]{1,0:T(1,128)} %copy-done.41) | copy-start | bytes 3076
  344.6 32.1 %copy-start.44 = (f32[1,256]{1,0:T(1,128)S(1)}, f32[1,256]{1,0:T(1,128)}, u32[]{:S(2)}) copy-start(f32[1,256]{1,0:T(1,128)} %copy-done.43) | copy-start | bytes 3076
  344.6 32.1 %copy-start.46 = (f32[1,256]{1,0:T(1,128)S(1)}, f32[1,256]{1,0:T(1,128)}, u32[]{:S(2)}) copy-start(f32[1,256]{1,0:T(1,128)} %copy-done.45) | copy-start | bytes 3076
  371.2 5.5 %collective-permute-start.3 = (f32[3,256]{1,0:T(4,128)S(1)}, f32[3,256]{1,0:T(4,128)S(1)}, u32[]{:S(2)}, u32[]{:S(2)}) collective-permute-start(f32[3,256]{1,0:T(4,128)S(1)} %slice.170), channel_id=1, source_target_pairs={{4,0},{8,4},{12,8},{16,12},{20,16},{24,20},{28,24},{5,1},{9,5},{13... | collective-permute-start | bytes 9224 | tf_op jit(solution)/shard_map/ppermute | solution.py:10
  (34 other events, 109.2 us)
Sparse Core Ops, SparseCore 0:
  24.7 125.4 all-gather.7
  197.0 123.3 all-gather.5
  339.9 30.1 all-reduce.2
where the time goes:
time: 386 us; the launch traced here: 384 us
  waiting for transfers between devices  231 us (60%)
  other arithmetic  48.1 us (12%)
  local copies, waits for them, and re-layouts  34.4 us (9%)
  matrix products  23.5 us (6%)
  blocking collectives  18.7 us (5%)
  between operations  15.9 us (4%)
  starting transfers between devices  11.8 us (3%)
    all_gather x2, waiting for transfers between devices, entering_2(): pieces = jax.tree.map(lambda part: lax.all_gather(part, axis), value)  207 us
    dot_general x10, matrix products, contract(): jnp.einsum(pattern, first_op, second_op, preferred_element_type=jnp.float32)  22.8 us
    psum x1, waiting for transfers between devices, body(): grad_bc_pre = lax.psum(grad_bc, 'head') * silu_grad(bc_pre)  22.7 us
    select_n x14, other arithmetic, step(): jnp.where(position < mine, new, old)  20.4 us
    unnamed x1, blocking collectives  18.7 us
    ppermute x4, starting transfers between devices, shifted(): return lax.ppermute(x, axis, pairs)  11.7 us
    mul x14, local copies, waits for them, and re-layouts, compose(): later[0][:, None, None] * earlier[1] + later[1]  9.59 us
    rev x2, local copies, waits for them, and re-layouts, entering_2(): pieces = jax.tree.map(lambda part: part[::-1], pieces)  8.89 us
  transfers between devices with their start and end apart: 7, of which 4 were waited for; matrix products, arithmetic and copies ran while one was open for 9% of the time, Pallas kernels for 0%

commit v1 on v0

v1 whole, which is shorter than its diff:
```python
import functools

import jax
import jax.numpy as jnp
from jax import lax
from jax.experimental import pallas as pl
from jax.experimental.pallas import tpu as pltpu
from jax.sharding import PartitionSpec as P

F32 = jnp.float32
BF16 = jnp.bfloat16
LANES = 128
RIM = 16


def dot_nn(a, b):
    return lax.dot_general(a, b, (((1,), (0,)), ((), ())), preferred_element_type=F32)


def dot_nt(a, b):
    return lax.dot_general(a, b, (((1,), (1,)), ((), ())), preferred_element_type=F32)


def dot_tn(a, b):
    return lax.dot_general(a, b, (((0,), (0,)), ((), ())), preferred_element_type=F32)


def exact_nn(a, b):
    return lax.dot_general(
        a, b, (((1,), (0,)), ((), ())), precision=lax.Precision.HIGHEST, preferred_element_type=F32
    )


def halves(value):
    top = value.astype(BF16)
    return top, (value - top.astype(F32)).astype(BF16)


def sigmoid(v):
    return 1.0 / (1.0 + jnp.exp(-v))


def kernel(
    n_ctx, n_head, pairs,
    x_ref, bc_ref, wx_ref, wbc_ref, dt_ref, alog_ref, dskip_ref, doc_ref, dy_ref,
    y_ref, gx_ref, gbc_ref, gdt_ref,
    halo_x, halo_bc, xp, bcp, stat, s_ref, g_ref, cexp, fin, fout, bin_, bout,
    xc, sx, lx, edy, sgrad, intra, dsc, step_l, leave_l, enter_l, gp, gbp, sgrad_bc,
    b_mat, c_mat, gram, bias, dgram, gb_acc, gc_acc, rr, cs, parts, nxt_x, nxt_bc,
    hx_send, hx_recv, hb_send, hb_recv, f_send, f_recv, b_send, b_recv,
    p_send, p_recv, nx_send, nx_recv, nb_send, nb_recv,
):
    rows = x_ref.shape[0]
    heads = dt_ref.shape[0]
    nstate = bc_ref.shape[1] // 2
    taps = wx_ref.shape[0]
    ctx = lax.axis_index("ctx")
    head = lax.axis_index("head")
    has_prev = ctx > 0
    has_next = ctx < n_ctx - 1
    half = LANES // 2

    barrier = pltpu.get_barrier_semaphore()

    @pl.when(has_prev)
    def _():
        pl.semaphore_signal(barrier, inc=1, device_id=(ctx - 1, head), device_id_type=pl.DeviceIdType.MESH)

    @pl.when(has_next)
    def _():
        pl.semaphore_signal(barrier, inc=1, device_id=(ctx + 1, head), device_id_type=pl.DeviceIdType.MESH)

    for off in range(1, n_head):
        pl.semaphore_signal(
            barrier, inc=1, device_id=(ctx, lax.rem(head + off, n_head)), device_id_type=pl.DeviceIdType.MESH
        )

    inside = has_prev & has_next

    @pl.when(inside)
    def _():
        pl.semaphore_wait(barrier, n_head + 1)

    @pl.when(jnp.logical_not(inside))
    def _():
        pl.semaphore_wait(barrier, n_head)

    def remote(src, dst, send, recv, to):
        return pltpu.make_async_remote_copy(
            src_ref=src, dst_ref=dst, send_sem=send, recv_sem=recv, device_id=to,
            device_id_type=pl.DeviceIdType.MESH,
        )

    after = (ctx + 1, head)
    before = (ctx - 1, head)
    x_halo = remote(x_ref.at[pl.ds(rows - RIM, RIM)], halo_x, hx_send, hx_recv, after)
    bc_halo = remote(bc_ref.at[pl.ds(rows - RIM, RIM)], halo_bc, hb_send, hb_recv, after)

    @pl.when(has_next)
    def _():
        bc_halo.start()
        x_halo.start()

    doc = doc_ref[0]
    dt = dt_ref[...]
    step = jnp.maximum(dt, 0.0) + jnp.log(1.0 + jnp.exp(-jnp.abs(dt)))
    decay = jnp.exp(alog_ref[...])
    r_id = lax.broadcasted_iota(jnp.int32, (rows, rows), 0)
    c_id = lax.broadcasted_iota(jnp.int32, (rows, rows), 1)
    same = (r_id >= doc) == (c_id >= doc)
    bias[...] = jnp.where(same & (r_id >= c_id), 0.0, -1e30)
    cum = exact_nn(-decay * step, jnp.where(r_id <= c_id, 1.0, 0.0))
    pos = lax.broadcasted_iota(jnp.int32, (heads, rows), 1)
    part = pos >= doc
    last_part = (rows - 1) >= doc
    enter = jnp.where(part, 0.0, jnp.exp(cum))
    final = cum[:, rows - 1 :]
    leave = jnp.where(part == last_part, jnp.exp(final - cum), 0.0)
    for k in range(pairs):
        pick = slice(2 * k, 2 * k + 2)
        stat[k, 0:2, :] = cum[pick]
        stat[k, 2:4, :] = step[pick]
        stat[k, 4:6, :] = leave[pick]
        stat[k, 6:8, :] = enter[pick]
    dgram[...] = jnp.zeros_like(dgram)
    gb_acc[...] = jnp.zeros_like(gb_acc)
    gc_acc[...] = jnp.zeros_like(gc_acc)

    @pl.when(has_next)
    def _():
        bc_halo.wait_send()
        x_halo.wait_send()

    @pl.when(has_prev)
    def _():
        bc_halo.wait_recv()
        x_halo.wait_recv()

    @pl.when(jnp.logical_not(has_prev))
    def _():
        halo_x[...] = jnp.zeros_like(halo_x)
        halo_bc[...] = jnp.zeros_like(halo_bc)
        fin[...] = jnp.zeros_like(fin)

    @pl.when(jnp.logical_not(has_next))
    def _():
        nxt_x[...] = jnp.zeros_like(nxt_x)
        nxt_bc[...] = jnp.zeros_like(nxt_bc)
        bin_[...] = jnp.zeros_like(bin_)

    def conv(pad_ref, weight):
        total = weight[0:1] * pad_ref[9 - taps : 9 - taps + rows, :]
        for tap in range(1, taps):
            at = 9 - taps + tap
            total = total + weight[tap : tap + 1] * pad_ref[at : at + rows, :]
        return total

    bcp[0:8, :] = halo_bc[RIM - 8 :, :].astype(F32)
    bcp[8:, :] = bc_ref[...].astype(F32)
    bc_pre = conv(bcp, wbc_ref[...].astype(F32))
    sig = sigmoid(bc_pre)
    bc_conv = (bc_pre * sig).astype(BF16)
    sgrad_bc[...] = sig * (1.0 + bc_pre * (1.0 - sig))
    b_mat[...] = bc_conv[:, :nstate]
    c_mat[...] = bc_conv[:, nstate:]
    gram[...] = dot_nt(bc_conv[:, nstate:], bc_conv[:, :nstate])

    lane = lax.broadcasted_iota(jnp.int32, (rows, LANES), 1)
    low = lane < half
    carry_on = doc >= rows

    def spread(columns, at):
        return jnp.where(low, columns[:, at : at + 1], columns[:, at + 1 : at + 2])

    def prepare(k):
        cols = pl.ds(pl.multiple_of(k * LANES, LANES), LANES)
        turned = jnp.transpose(stat[k])
        step_k = spread(turned, 2)
        leave_k = spread(turned, 4)
        enter_k = spread(turned, 6)
        step_l[:, cols] = step_k
        leave_l[:, cols] = leave_k
        enter_l[:, cols] = enter_k
        xp[0:8, :] = halo_x[RIM - 8 :, cols].astype(F32)
        xp[8:, :] = x_ref[:, cols].astype(F32)
        pre = conv(xp, wx_ref[:, cols].astype(F32))
        sig_k = sigmoid(pre)
        sgrad[:, cols] = sig_k * (1.0 + pre * (1.0 - sig_k))
        xb = (pre * sig_k).astype(BF16)
        xc[:, cols] = xb
        xf = xb.astype(F32)
        sx[:, cols] = (xf * step_k).astype(BF16)
        lx_k = (xf * (leave_k * step_k)).astype(BF16)
        lx[:, cols] = lx_k
        edy_k = (dy_ref[:, cols].astype(F32) * enter_k).astype(BF16)
        edy[:, cols] = edy_k
        s_ref[k] = dot_tn(lx_k, b_mat[...])
        g_ref[k] = dot_tn(edy_k, c_mat[...])
        ends = jnp.where(carry_on, jnp.exp(turned[rows - 1 : rows, 0:2]), 0.0)
        cexp[k, 0:half, :] = jnp.broadcast_to(ends[:, 0:1], (half, LANES))
        cexp[k, half:, :] = jnp.broadcast_to(ends[:, 1:2], (half, LANES))

    def chain(i):
        kf = i - ctx

        @pl.when((kf >= 0) & (kf < pairs))
        def _():
            @pl.when(has_prev)
            def _():
                remote(fout.at[kf], fin.at[kf], f_send.at[kf], f_recv.at[kf], after).wait_recv()

            @pl.when(has_next)
            def _():
                fout[kf] = (fin[kf].astype(F32) * cexp[kf] + s_ref[kf]).astype(BF16)
                remote(fout.at[kf], fin.at[kf], f_send.at[kf], f_recv.at[kf], after).start()

        kb = i - (n_ctx - 1 - ctx)

        @pl.when((kb >= 0) & (kb < pairs))
        def _():
            @pl.when(has_next)
            def _():
                remote(bout.at[kb], bin_.at[kb], b_send.at[kb], b_recv.at[kb], before).wait_recv()

            @pl.when(has_prev)
            def _():
                bout[kb] = (bin_[kb].astype(F32) * cexp[kb] + g_ref[kb]).astype(BF16)
                remote(bout.at[kb], bin_.at[kb], b_send.at[kb], b_recv.at[kb], before).start()

    def heavy(k):
        cols = pl.ds(pl.multiple_of(k * LANES, LANES), LANES)
        turned = jnp.transpose(stat[k])
        sx_k = sx[:, cols]
        dy_k = dy_ref[:, cols]
        zero = jnp.zeros_like(sx_k)
        outs, backs, weighs = [], [], []
        for j in range(2):
            mine = low if j == 0 else jnp.logical_not(low)
            ker = jnp.exp((turned[:, j : j + 1] - stat[k, j : j + 1, :]) + bias[...])
            mixing = (gram[...] * ker).astype(BF16)
            response = dot_nt(dy_k, jnp.where(mine, sx_k, zero))
            weighs.append(response * ker)
            outs.append(dot_nn(mixing, sx_k))
            backs.append(dot_tn(mixing, dy_k))
        dgram[...] += weighs[0] + weighs[1]
        intra[:, cols] = jnp.where(low, outs[0], outs[1])
        dsc[:, cols] = jnp.where(low, backs[0], backs[1])

    @pl.loop(0, pairs + n_ctx - 1)
    def _(i):
        @pl.when(i < pairs)
        def _():
            prepare(i)

        chain(i)

        @pl.when(i < pairs)
        def _():
            heavy(i)

    e_row = lax.broadcasted_iota(jnp.int32, (8, LANES), 0)
    e_col = lax.broadcasted_iota(jnp.int32, (8, LANES), 1) // half

    def finish(k):
        cols = pl.ds(pl.multiple_of(k * LANES, LANES), LANES)
        st = fin[k]
        ds = bin_[k]
        skip = dskip_ref[:, cols]
        step_k = step_l[:, cols]
        leave_k = leave_l[:, cols]
        xf = xc[:, cols].astype(F32)
        dyf = dy_ref[:, cols].astype(F32)
        dsc_k = dsc[:, cols]
        y_all = intra[:, cols] + enter_l[:, cols] * dot_nt(c_mat[...], st)
        y_ref[:, cols] = (y_all + skip * xf).astype(BF16)
        dlv = leave_k * dot_nt(b_mat[...], ds)
        both = dsc_k + dlv
        gp[0:rows, cols] = (step_k * both + skip * dyf) * sgrad[:, cols]
        gc_acc[...] += dot_nn(edy[:, cols], st)
        gb_acc[...] += dot_nn(lx[:, cols], ds)
        lterm = step_k * xf * dlv
        u1 = dyf * y_all - sx[:, cols].astype(F32) * dsc_k - lterm
        total = jnp.zeros((8, rows), F32)
        for at, value in ((0, u1), (2, xf * both), (4, lterm)):
            ones = jnp.where(e_row == e_col + at, 1.0, 0.0).astype(BF16)
            top, rest = halves(value)
            total = total + (dot_nt(ones, top) + dot_nt(ones, rest))
        rr[k] = total
        both_states = st.astype(F32) * ds.astype(F32) * cexp[k]
        cs[k, 0:1, :] = jnp.sum(both_states[0:half], axis=0, keepdims=True)
        cs[k, 1:2, :] = jnp.sum(both_states[half:], axis=0, keepdims=True)

    pl.loop(0, pairs)(finish)

    x_rim = remote(gp.at[pl.ds(0, 8)], nxt_x, nx_send, nx_recv, before)

    @pl.when(has_prev)
    def _():
        x_rim.start()

    top, rest = halves(dgram[...])
    grad_c = gc_acc[...] + dot_nn(top, b_mat[...]) + dot_nn(rest, b_mat[...])
    grad_b = gb_acc[...] + dot_tn(top, c_mat[...]) + dot_tn(rest, c_mat[...])
    parts[head, :, 0:nstate] = grad_b.astype(BF16)
    parts[head, :, nstate:] = grad_c.astype(BF16)
    sends = []
    for off in range(1, n_head):
        to = (ctx, lax.rem(head + off, n_head))
        copy = remote(parts.at[head], parts.at[head], p_send.at[off - 1], p_recv.at[off - 1], to)
        copy.start()
        sends.append(copy)

    tri = jnp.where(r_id >= c_id, 1.0, 0.0)
    dt_sig = sigmoid(dt)
    pos2 = lax.broadcasted_iota(jnp.int32, (2, rows), 1) == rows - 1
    cums, direct = [], []
    for k in range(pairs):
        extra = jnp.sum(rr[k, 4:6, :], axis=1, keepdims=True) + jnp.sum(cs[k, 0:2, :], axis=1, keepdims=True)
        cums.append(rr[k, 0:2, :] + jnp.where(pos2, extra, 0.0))
        direct.append(rr[k, 2:4, :])
    d_log = exact_nn(jnp.concatenate(cums, axis=0), tri)
    gdt_ref[...] = (jnp.concatenate(direct, axis=0) - decay * d_log) * dt_sig

    @pl.when(has_next)
    def _():
        x_rim.wait_recv()

    gp[rows:, :] = nxt_x[...]

    @pl.loop(0, pairs)
    def _(k):
        cols = pl.ds(pl.multiple_of(k * LANES, LANES), LANES)
        weight = wx_ref[:, cols].astype(F32)
        total = weight[taps - 1 : taps] * gp[0:rows, cols]
        for off in range(1, taps):
            total = total + weight[taps - 1 - off : taps - off] * gp[off : off + rows, cols]
        gx_ref[:, cols] = total.astype(BF16)

    for off in range(1, n_head):
        source = lax.rem(head + n_head - off, n_head)
        remote(
            parts.at[source], parts.at[source], p_send.at[off - 1], p_recv.at[off - 1],
            (ctx, lax.rem(head + off, n_head)),
        ).wait_recv()
    total = parts[0].astype(F32)
    for other in range(1, n_head):
        total = total + parts[other].astype(F32)
    gbp[0:rows, :] = total * sgrad_bc[...]
    bc_rim = remote(gbp.at[pl.ds(0, 8)], nxt_bc, nb_send, nb_recv, before)

    @pl.when(has_prev)
    def _():
        bc_rim.start()

    for copy in sends:
        copy.wait_send()

    @pl.loop(0, pairs)
    def _(k):
        @pl.when(has_next)
        def _():
            remote(fout.at[k], fin.at[k], f_send.at[k], f_recv.at[k], after).wait_send()

        @pl.when(has_prev)
        def _():
            remote(bout.at[k], bin_.at[k], b_send.at[k], b_recv.at[k], before).wait_send()

    @pl.when(has_next)
    def _():
        bc_rim.wait_recv()

    gbp[rows:, :] = nxt_bc[...]
    weight = wbc_ref[...].astype(F32)
    total = weight[taps - 1 : taps] * gbp[0:rows, :]
    for off in range(1, taps):
        total = total + weight[taps - 1 - off : taps - off] * gbp[off : off + rows, :]
    gbc_ref[...] = total.astype(BF16)

    @pl.when(has_prev)
    def _():
        x_rim.wait_send()
        bc_rim.wait_send()


def body(n_ctx, n_head, x_raw, bc_raw, conv_x_w, conv_bc_w, dt_raw, a_log, d_skip, doc_starts, grad_y):
    rows, channels = x_raw.shape
    heads = a_log.shape[0]
    nstate = bc_raw.shape[1] // 2
    pairs = channels // LANES
    vmem = pl.BlockSpec(memory_space=pltpu.VMEM)
    smem = pl.BlockSpec(memory_space=pltpu.SMEM)
    wide = pltpu.VMEM((rows, channels), F32)
    wide_h = pltpu.VMEM((rows, channels), BF16)
    state = pltpu.VMEM((pairs, LANES, nstate), F32)
    state_h = pltpu.VMEM((pairs, LANES, nstate), BF16)
    dma = pltpu.SemaphoreType.DMA
    scratch = [
        pltpu.VMEM((RIM, channels), BF16),
        pltpu.VMEM((RIM, 2 * nstate), BF16),
        pltpu.VMEM((rows + 8, LANES), F32),
        pltpu.VMEM((rows + 8, 2 * nstate), F32),
        pltpu.VMEM((pairs, 8, rows), F32),
        state, state, state,
        state_h, state_h, state_h, state_h,
        wide_h, wide_h, wide_h, wide_h,
        wide, wide, wide, wide, wide, wide,
        pltpu.VMEM((rows + 8, channels), F32),
        pltpu.VMEM((rows + 8, 2 * nstate), F32),
        pltpu.VMEM((rows, 2 * nstate), F32),
        pltpu.VMEM((rows, nstate), BF16),
        pltpu.VMEM((rows, nstate), BF16),
        pltpu.VMEM((rows, rows), F32),
        pltpu.VMEM((rows, rows), F32),
        pltpu.VMEM((rows, rows), F32),
        pltpu.VMEM((rows, nstate), F32),
        pltpu.VMEM((rows, nstate), F32),
        pltpu.VMEM((pairs, 8, rows), F32),
        pltpu.VMEM((pairs, 8, LANES), F32),
        pltpu.VMEM((n_head, rows, 2 * nstate), BF16),
        pltpu.VMEM((8, channels), F32),
        pltpu.VMEM((8, 2 * nstate), F32),
        dma, dma, dma, dma,
        dma((pairs,)), dma((pairs,)), dma((pairs,)), dma((pairs,)),
        dma((n_head - 1,)), dma((n_head - 1,)),
        dma, dma, dma, dma,
    ]
    return pl.pallas_call(
        functools.partial(kernel, n_ctx, n_head, pairs),
        out_shape=(
            jax.ShapeDtypeStruct((rows, channels), BF16),
            jax.ShapeDtypeStruct((rows, channels), BF16),
            jax.ShapeDtypeStruct((rows, 2 * nstate), BF16),
            jax.ShapeDtypeStruct((heads, rows), F32),
        ),
        in_specs=[vmem] * 7 + [smem, vmem],
        out_specs=(vmem, vmem, vmem, vmem),
        scratch_shapes=scratch,
        compiler_params=pltpu.CompilerParams(
            collective_id=0, has_side_effects=True, vmem_limit_bytes=56 * 1024 * 1024
        ),
        cost_estimate=pl.CostEstimate(flops=3 * 10**9, bytes_accessed=6 * 2**20, transcendentals=3 * 10**6),
    )(
        x_raw, bc_raw, conv_x_w, conv_bc_w, dt_raw, a_log[:, None],
        jnp.repeat(d_skip, channels // heads)[None, :], doc_starts, grad_y,
    )


def solution(mesh):
    in_specs = (
        P("ctx", "head"),
        P("ctx", None),
        P(None, "head"),
        P(),
        P("head", "ctx"),
        P("head"),
        P("head"),
        P("ctx"),
        P("ctx", "head"),
    )
    out_specs = (P("ctx", "head"), P("ctx", "head"), P("ctx", None), P("head", "ctx"))
    inner = functools.partial(body, mesh.shape["ctx"], mesh.shape["head"])
    return jax.shard_map(inner, mesh=mesh, in_specs=in_specs, out_specs=out_specs, check_vma=False)
```

time: 386 us -> 105 us (0.27)
  waiting for transfers between devices: 231 us -> 0 us
  Pallas kernels: 0 us -> 95.8 us
  other arithmetic: 48.1 us -> 0 us
  local copies, waits for them, and re-layouts: 34.4 us -> 6.88 us
  matrix products: 23.5 us -> 0 us
  blocking collectives: 18.7 us -> 0 us
  between operations: 15.9 us -> 1.31 us
  starting transfers between devices: 11.8 us -> 0 us
    all_gather x2 -> x0, waiting for transfers between devices: 207 us -> none  [entering_2(): pieces = jax.tree.map(lambda part: lax.all_gather(part, axis), value)]
    pallas_call x0 -> x1, Pallas kernels: none -> 95.8 us  [body(): pl.pallas_call(functools.partial(kernel, n_ctx, n_head, pairs), out_shape...]
    dot_general x12 -> x0, matrix products: 23.5 us -> none  [the longest x10 22.8 us: contract(): jnp.einsum(pattern, first_op, second_op, preferred_element_type=jnp.float32)]
    psum x1 -> x0, waiting for transfers between devices: 22.7 us -> none  [body(): grad_bc_pre = lax.psum(grad_bc, 'head') * silu_grad(bc_pre)]
    select_n x14 -> x0, other arithmetic: 20.4 us -> none  [step(): jnp.where(position < mine, new, old)]
    unnamed x1 -> x0, blocking collectives: 18.7 us -> none
    ppermute x4 -> x0, starting transfers between devices: 11.7 us -> none  [shifted(): return lax.ppermute(x, axis, pairs)]
    mul x14 -> x0, local copies, waits for them, and re-layouts: 9.59 us -> none  [compose(): later[0][:, None, None] * earlier[1] + later[1]]
  transfers between devices with their start and end apart: 7 -> 0, of which waited for: 4 -> 0; matrix products, arithmetic and copies ran while one was open for 9% -> 0% of each run, Pallas kernels for 0% -> 0%
where the time goes in v1:
time: 105 us; the launch traced here: 104 us
  Pallas kernels  95.8 us (91%)
  local copies, waits for them, and re-layouts  6.88 us (7%)
  between operations  1.31 us (1%)
    pallas_call x1, Pallas kernels, body(): pl.pallas_call(functools.partial(kernel, n_ctx, n_head, pairs), out_shape...  95.8 us
    unnamed x14, local copies, waits for them, and re-layouts  5.44 us

profile of v1, /device:TPU:0, one launch (start us, length us, event | category | flops | bytes accessed | tf_op | source)
XLA Modules:
  0.0 104.0 jit_solution(18122858941283852174)
XLA Ops:
  1.3 0.0 copy-start.3
  1.3 0.6 copy-done.3
  1.9 0.0 copy-start.4
  1.9 0.7 copy.13.alog_ref
  2.6 0.0 copy-done.4
  2.6 0.1 broadcast_in_dim.7
  2.7 0.7 broadcast_in_dim_reshape.3.dskip_ref
  3.4 95.8 %shard_map.120 = (bf16[256,2048]{1,0:T(8,128)(2,1)}, bf16[256,2048]{1,0:T(8,128)(2,1)}, bf16[256,256]{1,0:T(8,128)(2,1)}, f32[32,256]{1,0:T(8,128)}) custom-call(bf16[256,2048]{1,0:T(8,128)(2,1)} %x_ref.1, bf16[256,256]{1,0:T(8,128)(2,1)} %bc_ref.1, bf16[4,2048]{1,0:T(4,128)(2,1)} %wx_ref.1, bf16[4,256]{1,0:T(4,128)(2,1)} %wbc_ref.1, f32[32,256]{1,0:T(8,128)} %dt_ref.1, ...), custom_call_target="tpu_custom_call" | custom-call | flops 3000000000 | bytes 6291456 | tf_op jit(solution)/shard_map/pallas_call | solution.py:427
  99.2 0.0 copy-start
  99.2 2.4 %copy.19 = bf16[256,2048]{1,0:T(8,128)(2,1)} copy(bf16[256,2048]{1,0:T(8,128)(2,1)} %get-tuple-element.8) | data formatting | bytes 2097152
  101.6 0.0 copy-done
  101.6 0.0 copy-start.1
  101.6 1.0 copy.20
  102.6 0.1 copy-done.1
  102.6 0.0 copy-start.2
  102.6 0.7 copy.21
  103.3 0.1 copy-done.2
  103.4 0.6 copy.22
Async XLA Ops:
  1.3 0.7 copy-start.3
  1.9 0.7 copy-start.4
  99.2 2.4 %copy-start = (bf16[256,2048]{1,0:T(8,128)(2,1)S(1)}, bf16[256,2048]{1,0:T(8,128)(2,1)}, u32[]{:S(2)}) copy-start(bf16[256,2048]{1,0:T(8,128)(2,1)} %get-tuple-element.9) | copy-start | bytes 3145732
  101.6 1.0 copy-start.1
  102.6 0.8 copy-start.2

commit v2 on v1

--- a/solution.py
+++ b/solution.py
@@ -11,6 +11,7 @@
 BF16 = jnp.bfloat16
 LANES = 128
 RIM = 16
+LAG = 2
 
 
 def dot_nn(a, b):
@@ -44,10 +45,12 @@
     n_ctx, n_head, pairs,
     x_ref, bc_ref, wx_ref, wbc_ref, dt_ref, alog_ref, dskip_ref, doc_ref, dy_ref,
     y_ref, gx_ref, gbc_ref, gdt_ref,
-    halo_x, halo_bc, xp, bcp, stat, s_ref, g_ref, cexp, fin, fout, bin_, bout,
+    halo_x, halo_bc, xp, bcp, stat, s_ref, g_ref, carry_own, carry_oth,
+    s_out, s_in, g_out, g_in, fin, fout, bin_, bout, z_in, z_out, r_in, r_out,
     xc, sx, lx, edy, sgrad, intra, dsc, step_l, leave_l, enter_l, gp, gbp, sgrad_bc,
     b_mat, c_mat, gram, bias, dgram, gb_acc, gc_acc, rr, cs, parts, nxt_x, nxt_bc,
-    hx_send, hx_recv, hb_send, hb_recv, f_send, f_recv, b_send, b_recv,
+    hx_send, hx_recv, hb_send, hb_recv, f_send, f_recv, b_send, b_recv, c_send, c_recv,
+    s_send, s_recv, g_send, g_recv, z_send, z_recv, r_send, r_recv,
     p_send, p_recv, nx_send, nx_recv, nb_send, nb_recv,
 ):
     rows = x_ref.shape[0]
@@ -62,28 +65,29 @@
 
     barrier = pltpu.get_barrier_semaphore()
 
-    @pl.when(has_prev)
-    def _():
-        pl.semaphore_signal(barrier, inc=1, device_id=(ctx - 1, head), device_id_type=pl.DeviceIdType.MESH)
-
-    @pl.when(has_next)
-    def _():
-        pl.semaphore_signal(barrier, inc=1, device_id=(ctx + 1, head), device_id_type=pl.DeviceIdType.MESH)
+    for dist in (1, 2):
+        for sign in (-1, 1):
+
+            @pl.when((ctx + sign * dist >= 0) & (ctx + sign * dist < n_ctx))
+            def _(dist=dist, sign=sign):
+                pl.semaphore_signal(
+                    barrier, inc=1, device_id=(ctx + sign * dist, head), device_id_type=pl.DeviceIdType.MESH
+                )
 
     for off in range(1, n_head):
         pl.semaphore_signal(
             barrier, inc=1, device_id=(ctx, lax.rem(head + off, n_head)), device_id_type=pl.DeviceIdType.MESH
         )
 
-    inside = has_prev & has_next
-
-    @pl.when(inside)
-    def _():
-        pl.semaphore_wait(barrier, n_head + 1)
-
-    @pl.when(jnp.logical_not(inside))
-    def _():
-        pl.semaphore_wait(barrier, n_head)
+    for lows in range(3):
+        for highs in range(3):
+            is_low = ctx == lows if lows < 2 else ctx >= 2
+            left = n_ctx - 1 - ctx
+            is_high = left == highs if highs < 2 else left >= 2
+
+            @pl.when(is_low & is_high)
+            def _(count=lows + highs + n_head - 1):
+                pl.semaphore_wait(barrier, count)
 
     def remote(src, dst, send, recv, to):
         return pltpu.make_async_remote_copy(
@@ -93,6 +97,16 @@
 
     after = (ctx + 1, head)
     before = (ctx - 1, head)
+    side = lax.rem(ctx, 2)
+    first = side == 0
+    duo = ctx // 2
+    duos = n_ctx // 2
+    partner = (ctx + 1 - 2 * side, head)
+    z_next = (ctx + 2, head)
+    z_prev = (ctx - 2, head)
+    has_up = duo > 0
+    has_down = duo < duos - 1
+    own_count = pairs // 2
     x_halo = remote(x_ref.at[pl.ds(rows - RIM, RIM)], halo_x, hx_send, hx_recv, after)
     bc_halo = remote(bc_ref.at[pl.ds(rows - RIM, RIM)], halo_bc, hb_send, hb_recv, after)
 
@@ -104,7 +118,11 @@
     doc = doc_ref[0]
     dt = dt_ref[...]
     step = jnp.maximum(dt, 0.0) + jnp.log(1.0 + jnp.exp(-jnp.abs(dt)))
-    decay = jnp.exp(alog_ref[...])
+    head_id = lax.broadcasted_iota(jnp.int32, (heads, LANES), 0)
+    logs = jnp.zeros((heads, LANES), F32)
+    for h in range(heads):
+        logs = jnp.where(head_id == h, alog_ref[h], logs)
+    decay = jnp.exp(logs)[:, 0:1]
     r_id = lax.broadcasted_iota(jnp.int32, (rows, rows), 0)
     c_id = lax.broadcasted_iota(jnp.int32, (rows, rows), 1)
     same = (r_id >= doc) == (c_id >= doc)
@@ -122,9 +140,11 @@
         stat[k, 2:4, :] = step[pick]
         stat[k, 4:6, :] = leave[pick]
         stat[k, 6:8, :] = enter[pick]
+    ends = jnp.where(doc >= rows, jnp.exp(final), 0.0)
+    carry_own[...] = jnp.broadcast_to(ends, (heads, LANES))
+    carry_copy = remote(carry_own, carry_oth, c_send, c_recv, partner)
+    carry_copy.start()
     dgram[...] = jnp.zeros_like(dgram)
-    gb_acc[...] = jnp.zeros_like(gb_acc)
-    gc_acc[...] = jnp.zeros_like(gc_acc)
 
     @pl.when(has_next)
     def _():
@@ -140,13 +160,19 @@
     def _():
         halo_x[...] = jnp.zeros_like(halo_x)
         halo_bc[...] = jnp.zeros_like(halo_bc)
-        fin[...] = jnp.zeros_like(fin)
 
     @pl.when(jnp.logical_not(has_next))
     def _():
         nxt_x[...] = jnp.zeros_like(nxt_x)
         nxt_bc[...] = jnp.zeros_like(nxt_bc)
-        bin_[...] = jnp.zeros_like(bin_)
+
+    @pl.when(jnp.logical_not(has_up))
+    def _():
+        z_in[...] = jnp.zeros_like(z_in)
+
+    @pl.when(jnp.logical_not(has_down))
+    def _():
+        r_in[...] = jnp.zeros_like(r_in)
 
     def conv(pad_ref, weight):
         total = weight[0:1] * pad_ref[9 - taps : 9 - taps + rows, :]
@@ -167,7 +193,6 @@
 
     lane = lax.broadcasted_iota(jnp.int32, (rows, LANES), 1)
     low = lane < half
-    carry_on = doc >= rows
 
     def spread(columns, at):
         return jnp.where(low, columns[:, at : at + 1], columns[:, at + 1 : at + 2])
@@ -194,38 +219,80 @@
         lx[:, cols] = lx_k
         edy_k = (dy_ref[:, cols].astype(F32) * enter_k).astype(BF16)
         edy[:, cols] = edy_k
-        s_ref[k] = dot_tn(lx_k, b_mat[...])
-        g_ref[k] = dot_tn(edy_k, c_mat[...])
-        ends = jnp.where(carry_on, jnp.exp(turned[rows - 1 : rows, 0:2]), 0.0)
-        cexp[k, 0:half, :] = jnp.broadcast_to(ends[:, 0:1], (half, LANES))
-        cexp[k, half:, :] = jnp.broadcast_to(ends[:, 1:2], (half, LANES))
+        s_k = dot_tn(lx_k, b_mat[...])
+        g_k = dot_tn(edy_k, c_mat[...])
+        s_ref[k] = s_k
+        g_ref[k] = g_k
+
+        @pl.when(lax.rem(k, 2) != side)
+        def _():
+            s_out[k] = s_k.astype(BF16)
+            remote(s_out.at[k], s_in.at[k], s_send.at[k], s_recv.at[k], partner).start()
+            g_out[k] = g_k.astype(BF16)
+            remote(g_out.at[k], g_in.at[k], g_send.at[k], g_recv.at[k], partner).start()
+
+    def carry_rows(ref, k):
+        return jnp.concatenate(
+            [jnp.broadcast_to(ref[pl.ds(2 * k + j, 1), :], (half, LANES)) for j in range(2)], axis=0
+        )
+
+    def lag(kind, q):
+        k = 2 * q + side
+        own, other = carry_rows(carry_own, k), carry_rows(carry_oth, k)
+        if kind == "z":
+            remote(s_out.at[k], s_in.at[k], s_send.at[k], s_recv.at[k], partner).wait_recv()
+
+            @pl.when(has_up)
+            def _():
+                remote(z_out.at[k], z_in.at[k], z_send.at[k], z_recv.at[k], z_next).wait_recv()
+
+            mine, theirs, enters = s_ref[k], s_in[k].astype(F32), z_in[k].astype(F32)
+            near = first
+        else:
+            remote(g_out.at[k], g_in.at[k], g_send.at[k], g_recv.at[k], partner).wait_recv()
+
+            @pl.when(has_down)
+            def _():
+                remote(r_out.at[k], r_in.at[k], r_send.at[k], r_recv.at[k], z_prev).wait_recv()
+
+            mine, theirs, enters = g_ref[k], g_in[k].astype(F32), r_in[k].astype(F32)
+            near = jnp.logical_not(first)
+        middle = jnp.where(near, own, other) * enters + jnp.where(near, mine, theirs)
+        leaves = jnp.where(near, other, own) * middle + jnp.where(near, theirs, mine)
+        keep = jnp.where(near, enters, middle).astype(BF16)
+        give = jnp.where(near, middle, enters).astype(BF16)
+        if kind == "z":
+
+            @pl.when(has_down)
+            def _():
+                z_out[k] = leaves.astype(BF16)
+                remote(z_out.at[k], z_in.at[k], z_send.at[k], z_recv.at[k], z_next).start()
+
+            fin[k] = keep
+            fout[k] = give
+            remote(fout.at[k], fin.at[k], f_send.at[k], f_recv.at[k], partner).start()
+        else:
+
+            @pl.when(has_up)
+            def _():
+                r_out[k] = leaves.astype(BF16)
+                remote(r_out.at[k], r_in.at[k], r_send.at[k], r_recv.at[k], z_prev).start()
+
+            bin_[k] = keep
+            bout[k] = give
+            remote(bout.at[k], bin_.at[k], b_send.at[k], b_recv.at[k], partner).start()
 
     def chain(i):
-        kf = i - ctx
-
-        @pl.when((kf >= 0) & (kf < pairs))
+        ahead = i - LAG * duo
+        back = i - LAG * (duos - 1 - duo)
+
+        @pl.when((ahead >= 0) & (ahead < own_count))
         def _():
-            @pl.when(has_prev)
-            def _():
-                remote(fout.at[kf], fin.at[kf], f_send.at[kf], f_recv.at[kf], after).wait_recv()
-
-            @pl.when(has_next)
-            def _():
-                fout[kf] = (fin[kf].astype(F32) * cexp[kf] + s_ref[kf]).astype(BF16)
-                remote(fout.at[kf], fin.at[kf], f_send.at[kf], f_recv.at[kf], after).start()
-
-        kb = i - (n_ctx - 1 - ctx)
-
-        @pl.when((kb >= 0) & (kb < pairs))
+            lag("z", ahead)
+
+        @pl.when((back >= 0) & (back < own_count))
         def _():
-            @pl.when(has_next)
-            def _():
-                remote(bout.at[kb], bin_.at[kb], b_send.at[kb], b_recv.at[kb], before).wait_recv()
-
-            @pl.when(has_prev)
-            def _():
-                bout[kb] = (bin_[kb].astype(F32) * cexp[kb] + g_ref[kb]).astype(BF16)
-                remote(bout.at[kb], bin_.at[kb], b_send.at[kb], b_recv.at[kb], before).start()
+            lag("r", back)
 
     def heavy(k):
         cols = pl.ds(pl.multiple_of(k * LANES, LANES), LANES)
@@ -246,57 +313,35 @@
         intra[:, cols] = jnp.where(low, outs[0], outs[1])
         dsc[:, cols] = jnp.where(low, backs[0], backs[1])
 
-    @pl.loop(0, pairs + n_ctx - 1)
+    pl.loop(0, pairs)(prepare)
+    carry_copy.wait_recv()
+
+    @pl.loop(0, max(pairs, own_count + LAG * (duos - 1)))
     def _(i):
-        @pl.when(i < pairs)
-        def _():
-            prepare(i)
-
         chain(i)
 
         @pl.when(i < pairs)
         def _():
             heavy(i)
 
-    e_row = lax.broadcasted_iota(jnp.int32, (8, LANES), 0)
-    e_col = lax.broadcasted_iota(jnp.int32, (8, LANES), 1) // half
-
-    def finish(k):
+    gb_acc[...] = jnp.zeros_like(gb_acc)
+    gc_acc[...] = jnp.zeros_like(gc_acc)
+
+    def project(k):
         cols = pl.ds(pl.multiple_of(k * LANES, LANES), LANES)
-        st = fin[k]
-        ds = bin_[k]
-        skip = dskip_ref[:, cols]
-        step_k = step_l[:, cols]
-        leave_k = leave_l[:, cols]
-        xf = xc[:, cols].astype(F32)
-        dyf = dy_ref[:, cols].astype(F32)
-        dsc_k = dsc[:, cols]
-        y_all = intra[:, cols] + enter_l[:, cols] * dot_nt(c_mat[...], st)
-        y_ref[:, cols] = (y_all + skip * xf).astype(BF16)
-        dlv = leave_k * dot_nt(b_mat[...], ds)
-        both = dsc_k + dlv
-        gp[0:rows, cols] = (step_k * both + skip * dyf) * sgrad[:, cols]
-        gc_acc[...] += dot_nn(edy[:, cols], st)
-        gb_acc[...] += dot_nn(lx[:, cols], ds)
-        lterm = step_k * xf * dlv
-        u1 = dyf * y_all - sx[:, cols].astype(F32) * dsc_k - lterm
-        total = jnp.zeros((8, rows), F32)
-        for at, value in ((0, u1), (2, xf * both), (4, lterm)):
-            ones = jnp.where(e_row == e_col + at, 1.0, 0.0).astype(BF16)
-            top, rest = halves(value)
-            total = total + (dot_nt(ones, top) + dot_nt(ones, rest))
-        rr[k] = total
-        both_states = st.astype(F32) * ds.astype(F32) * cexp[k]
-        cs[k, 0:1, :] = jnp.sum(both_states[0:half], axis=0, keepdims=True)
-        cs[k, 1:2, :] = jnp.sum(both_states[half:], axis=0, keepdims=True)
-
-    pl.loop(0, pairs)(finish)
-
-    x_rim = remote(gp.at[pl.ds(0, 8)], nxt_x, nx_send, nx_recv, before)
-
-    @pl.when(has_prev)
-    def _():
-        x_rim.start()
+        gc_acc[...] += dot_nn(edy[:, cols], fin[k])
+        gb_acc[...] += dot_nn(lx[:, cols], bin_[k])
+
+    @pl.loop(0, own_count)
+    def _(q):
+        project(2 * q + side)
+
+    @pl.loop(0, own_count)
+    def _(q):
+        k = 2 * q + 1 - side
+        remote(fout.at[k], fin.at[k], f_send.at[k], f_recv.at[k], partner).wait_recv()
+        remote(bout.at[k], bin_.at[k], b_send.at[k], b_recv.at[k], partner).wait_recv()
+        project(k)
 
     top, rest = halves(dgram[...])
     grad_c = gc_acc[...] + dot_nn(top, b_mat[...]) + dot_nn(rest, b_mat[...])
@@ -310,6 +355,44 @@
         copy.start()
         sends.append(copy)
 
+    e_row = lax.broadcasted_iota(jnp.int32, (8, LANES), 0)
+    e_col = lax.broadcasted_iota(jnp.int32, (8, LANES), 1) // half
+
+    def finish(k):
+        cols = pl.ds(pl.multiple_of(k * LANES, LANES), LANES)
+        st = fin[k]
+        ds = bin_[k]
+        skip = jnp.where(low[0:1], dskip_ref[2 * k], dskip_ref[2 * k + 1])
+        step_k = step_l[:, cols]
+        leave_k = leave_l[:, cols]
+        xf = xc[:, cols].astype(F32)
+        dyf = dy_ref[:, cols].astype(F32)
+        dsc_k = dsc[:, cols]
+        y_all = intra[:, cols] + enter_l[:, cols] * dot_nt(c_mat[...], st)
+        y_ref[:, cols] = (y_all + skip * xf).astype(BF16)
+        dlv = leave_k * dot_nt(b_mat[...], ds)
+        both = dsc_k + dlv
+        gp[0:rows, cols] = (step_k * both + skip * dyf) * sgrad[:, cols]
+        lterm = step_k * xf * dlv
+        u1 = dyf * y_all - sx[:, cols].astype(F32) * dsc_k - lterm
+        total = jnp.zeros((8, rows), F32)
+        for at, value in ((0, u1), (2, xf * both), (4, lterm)):
+            ones = jnp.where(e_row == e_col + at, 1.0, 0.0).astype(BF16)
+            top, rest = halves(value)
+            total = total + (dot_nt(ones, top) + dot_nt(ones, rest))
+        rr[k] = total
+        both_states = st.astype(F32) * ds.astype(F32) * carry_rows(carry_own, k)
+        cs[k, 0:1, :] = jnp.sum(both_states[0:half], axis=0, keepdims=True)
+        cs[k, 1:2, :] = jnp.sum(both_states[half:], axis=0, keepdims=True)
+
+    pl.loop(0, pairs)(finish)
+
+    x_rim = remote(gp.at[pl.ds(0, 8)], nxt_x, nx_send, nx_recv, before)
+
+    @pl.when(has_prev)
+    def _():
+        x_rim.start()
+
     tri = jnp.where(r_id >= c_id, 1.0, 0.0)
     dt_sig = sigmoid(dt)
     pos2 = lax.broadcasted_iota(jnp.int32, (2, rows), 1) == rows - 1
@@ -355,15 +438,24 @@
     for copy in sends:
         copy.wait_send()
 
-    @pl.loop(0, pairs)
-    def _(k):
-        @pl.when(has_next)
+    carry_copy.wait_send()
+
+    @pl.loop(0, own_count)
+    def _(q):
+        k = 2 * q + side
+        j = 2 * q + 1 - side
+        remote(s_out.at[j], s_in.at[j], s_send.at[j], s_recv.at[j], partner).wait_send()
+        remote(g_out.at[j], g_in.at[j], g_send.at[j], g_recv.at[j], partner).wait_send()
+        remote(fout.at[k], fin.at[k], f_send.at[k], f_recv.at[k], partner).wait_send()
+        remote(bout.at[k], bin_.at[k], b_send.at[k], b_recv.at[k], partner).wait_send()
+
+        @pl.when(has_down)
         def _():
-            remote(fout.at[k], fin.at[k], f_send.at[k], f_recv.at[k], after).wait_send()
-
-        @pl.when(has_prev)
+            remote(z_out.at[k], z_in.at[k], z_send.at[k], z_recv.at[k], z_next).wait_send()
+
+        @pl.when(has_up)
         def _():
-            remote(bout.at[k], bin_.at[k], b_send.at[k], b_recv.at[k], before).wait_send()
+            remote(r_out.at[k], r_in.at[k], r_send.at[k], r_recv.at[k], z_prev).wait_send()
 
     @pl.when(has_next)
     def _():
@@ -400,8 +492,10 @@
         pltpu.VMEM((rows + 8, LANES), F32),
         pltpu.VMEM((rows + 8, 2 * nstate), F32),
         pltpu.VMEM((pairs, 8, rows), F32),
-        state, state, state,
-        state_h, state_h, state_h, state_h,
+        state, state,
+        pltpu.VMEM((heads, LANES), F32),
+        pltpu.VMEM((heads, LANES), F32),
+        state_h, state_h, state_h, state_h, state_h, state_h, state_h, state_h, state_h, state_h, state_h, state_h,
         wide_h, wide_h, wide_h, wide_h,
         wide, wide, wide, wide, wide, wide,
         pltpu.VMEM((rows + 8, channels), F32),
@@ -420,6 +514,8 @@
         pltpu.VMEM((8, channels), F32),
         pltpu.VMEM((8, 2 * nstate), F32),
         dma, dma, dma, dma,
+        dma((pairs,)), dma((pairs,)), dma((pairs,)), dma((pairs,)), dma, dma,
+        dma((pairs,)), dma((pairs,)), dma((pairs,)), dma((pairs,)),
         dma((pairs,)), dma((pairs,)), dma((pairs,)), dma((pairs,)),
         dma((n_head - 1,)), dma((n_head - 1,)),
         dma, dma, dma, dma,
@@ -432,7 +528,7 @@
             jax.ShapeDtypeStruct((rows, 2 * nstate), BF16),
             jax.ShapeDtypeStruct((heads, rows), F32),
         ),
-        in_specs=[vmem] * 7 + [smem, vmem],
+        in_specs=[vmem] * 5 + [smem, smem, smem, vmem],
         out_specs=(vmem, vmem, vmem, vmem),
         scratch_shapes=scratch,
         compiler_params=pltpu.CompilerParams(
@@ -440,8 +536,7 @@
         ),
         cost_estimate=pl.CostEstimate(flops=3 * 10**9, bytes_accessed=6 * 2**20, transcendentals=3 * 10**6),
     )(
-        x_raw, bc_raw, conv_x_w, conv_bc_w, dt_raw, a_log[:, None],
-        jnp.repeat(d_skip, channels // heads)[None, :], doc_starts, grad_y,
+        x_raw, bc_raw, conv_x_w, conv_bc_w, dt_raw, a_log, d_skip, doc_starts, grad_y
     )
 
 

time: 105 us -> 70.3 us (0.67)
  Pallas kernels: 95.8 us -> 63.6 us
  local copies, waits for them, and re-layouts: 6.88 us -> 4.79 us
    pallas_call x1, Pallas kernels: 95.8 us -> 63.6 us  [body(): pl.pallas_call(functools.partial(kernel, n_ctx, n_head, pairs), out_shape...]
    unnamed x14 -> x10, local copies, waits for them, and re-layouts: 5.44 us -> 4.79 us
where the time goes in v2:
time: 70.3 us; the launch traced here: 69.7 us
  Pallas kernels  63.6 us (90%)
  local copies, waits for them, and re-layouts  4.79 us (7%)
  between operations  1.3 us (2%)
    pallas_call x1, Pallas kernels, body(): pl.pallas_call(functools.partial(kernel, n_ctx, n_head, pairs), out_shape...  63.6 us
    unnamed x10, local copies, waits for them, and re-layouts  4.79 us

profile of v2, /device:TPU:0, one launch (start us, length us, event | category | flops | bytes accessed | tf_op | source)
XLA Modules:
  0.0 69.7 jit_solution(7535779896078251323)
XLA Ops:
  1.3 63.6 %shard_map.120 = (bf16[256,2048]{1,0:T(8,128)(2,1)}, bf16[256,2048]{1,0:T(8,128)(2,1)}, bf16[256,256]{1,0:T(8,128)(2,1)}, f32[32,256]{1,0:T(8,128)}) custom-call(bf16[256,2048]{1,0:T(8,128)(2,1)} %x_ref.1, bf16[256,256]{1,0:T(8,128)(2,1)} %bc_ref.1, bf16[4,2048]{1,0:T(4,128)(2,1)} %wx_ref.1, bf16[4,256]{1,0:T(4,128)(2,1)} %wbc_ref.1, f32[32,256]{1,0:T(8,128)} %dt_ref.1, ...), custom_call_target="tpu_custom_call" | custom-call | flops 3000000000 | bytes 6291456 | tf_op jit(solution)/shard_map/pallas_call | solution.py:523
  64.9 0.0 copy-start
  64.9 2.4 %copy.18 = bf16[256,2048]{1,0:T(8,128)(2,1)} copy(bf16[256,2048]{1,0:T(8,128)(2,1)} %get-tuple-element.8) | data formatting | bytes 2097152
  67.3 0.0 copy-done
  67.3 0.0 copy-start.1
  67.3 1.0 %copy.19 = bf16[256,2048]{1,0:T(8,128)(2,1)} copy(bf16[256,2048]{1,0:T(8,128)(2,1)S(1)} %copy-done) | data formatting | bytes 2097152
  68.3 0.1 copy-done.1
  68.4 0.0 copy-start.2
  68.4 0.7 copy.20
  69.0 0.1 copy-done.2
  69.1 0.6 copy.21
Async XLA Ops:
  64.9 2.4 %copy-start = (bf16[256,2048]{1,0:T(8,128)(2,1)S(1)}, bf16[256,2048]{1,0:T(8,128)(2,1)}, u32[]{:S(2)}) copy-start(bf16[256,2048]{1,0:T(8,128)(2,1)} %get-tuple-element.9) | copy-start | bytes 3145732
  67.3 1.0 %copy-start.1 = (bf16[256,256]{1,0:T(8,128)(2,1)S(1)}, bf16[256,256]{1,0:T(8,128)(2,1)}, u32[]{:S(2)}) copy-start(bf16[256,256]{1,0:T(8,128)(2,1)} %get-tuple-element.10) | copy-start | bytes 393220
  68.4 0.8 %copy-start.2 = (f32[32,256]{1,0:T(8,128)S(1)}, f32[32,256]{1,0:T(8,128)}, u32[]{:S(2)}) copy-start(f32[32,256]{1,0:T(8,128)} %get-tuple-element.11) | copy-start | bytes 98308

commit v3 on v2

--- a/solution.py
+++ b/solution.py
@@ -12,6 +12,7 @@
 LANES = 128
 RIM = 16
 LAG = 2
+PIECES = 4
 
 
 def dot_nn(a, b):
@@ -38,7 +39,7 @@
 
 
 def sigmoid(v):
-    return 1.0 / (1.0 + jnp.exp(-v))
+    return 0.5 + 0.5 * jnp.tanh(0.5 * v)
 
 
 def kernel(
@@ -62,6 +63,7 @@
     has_prev = ctx > 0
     has_next = ctx < n_ctx - 1
     half = LANES // 2
+    mid = rows // 2
 
     barrier = pltpu.get_barrier_semaphore()
 
@@ -197,7 +199,7 @@
     def spread(columns, at):
         return jnp.where(low, columns[:, at : at + 1], columns[:, at + 1 : at + 2])
 
-    def prepare(k):
+    def prepare(k, slot):
         cols = pl.ds(pl.multiple_of(k * LANES, LANES), LANES)
         turned = jnp.transpose(stat[k])
         step_k = spread(turned, 2)
@@ -206,9 +208,10 @@
         step_l[:, cols] = step_k
         leave_l[:, cols] = leave_k
         enter_l[:, cols] = enter_k
-        xp[0:8, :] = halo_x[RIM - 8 :, cols].astype(F32)
-        xp[8:, :] = x_ref[:, cols].astype(F32)
-        pre = conv(xp, wx_ref[:, cols].astype(F32))
+        xp_k = xp.at[slot]
+        xp_k[0:8, :] = halo_x[RIM - 8 :, cols].astype(F32)
+        xp_k[8:, :] = x_ref[:, cols].astype(F32)
+        pre = conv(xp_k, wx_ref[:, cols].astype(F32))
         sig_k = sigmoid(pre)
         sgrad[:, cols] = sig_k * (1.0 + pre * (1.0 - sig_k))
         xb = (pre * sig_k).astype(BF16)
@@ -303,17 +306,28 @@
         outs, backs, weighs = [], [], []
         for j in range(2):
             mine = low if j == 0 else jnp.logical_not(low)
-            ker = jnp.exp((turned[:, j : j + 1] - stat[k, j : j + 1, :]) + bias[...])
-            mixing = (gram[...] * ker).astype(BF16)
-            response = dot_nt(dy_k, jnp.where(mine, sx_k, zero))
-            weighs.append(response * ker)
-            outs.append(dot_nn(mixing, sx_k))
-            backs.append(dot_tn(mixing, dy_k))
-        dgram[...] += weighs[0] + weighs[1]
-        intra[:, cols] = jnp.where(low, outs[0], outs[1])
-        dsc[:, cols] = jnp.where(low, backs[0], backs[1])
-
-    pl.loop(0, pairs)(prepare)
+            sx_j = jnp.where(mine, sx_k, zero)
+            column, row = turned[:, j : j + 1], stat[k, j : j + 1, :]
+            sources = []
+            for at, width in ((0, mid), (mid, rows)):
+                ker = jnp.exp((column[at : at + mid] - row[:, :width]) + bias[at : at + mid, :width])
+                mixing = (gram[at : at + mid, :width] * ker).astype(BF16)
+                weighs.append(dot_nt(dy_k[at : at + mid], sx_j[:width]) * ker)
+                outs.append(dot_nn(mixing, sx_k[:width]))
+                sources.append(dot_tn(mixing, dy_k[at : at + mid]))
+            backs.append((sources[1][:mid] + sources[0], sources[1][mid:]))
+        dgram[0:mid, 0:mid] += weighs[0] + weighs[2]
+        dgram[mid:, :] += weighs[1] + weighs[3]
+        for h in range(2):
+            rows_h = slice(h * mid, (h + 1) * mid)
+            intra[rows_h, cols] = jnp.where(low[:mid], outs[h], outs[2 + h])
+            dsc[rows_h, cols] = jnp.where(low[:mid], backs[0][h], backs[1][h])
+
+    @pl.loop(0, pairs // 2)
+    def _(k):
+        prepare(2 * k, 0)
+        prepare(2 * k + 1, 1)
+
     carry_copy.wait_recv()
 
     @pl.loop(0, max(pairs, own_count + LAG * (duos - 1)))
@@ -355,8 +369,10 @@
         copy.start()
         sends.append(copy)
 
-    e_row = lax.broadcasted_iota(jnp.int32, (8, LANES), 0)
-    e_col = lax.broadcasted_iota(jnp.int32, (8, LANES), 1) // half
+    e_row = lax.broadcasted_iota(jnp.int32, (3 * LANES, LANES), 0)
+    e_col = lax.broadcasted_iota(jnp.int32, (3 * LANES, LANES), 1)
+    e_at = (e_row % LANES) // half + jnp.where(e_row < 2 * LANES, 0, heads) - e_col
+    rr[...] = jnp.zeros_like(rr)
 
     def finish(k):
         cols = pl.ds(pl.multiple_of(k * LANES, LANES), LANES)
@@ -375,49 +391,27 @@
         gp[0:rows, cols] = (step_k * both + skip * dyf) * sgrad[:, cols]
         lterm = step_k * xf * dlv
         u1 = dyf * y_all - sx[:, cols].astype(F32) * dsc_k - lterm
-        total = jnp.zeros((8, rows), F32)
-        for at, value in ((0, u1), (2, xf * both), (4, lterm)):
-            ones = jnp.where(e_row == e_col + at, 1.0, 0.0).astype(BF16)
-            top, rest = halves(value)
-            total = total + (dot_nt(ones, top) + dot_nt(ones, rest))
-        rr[k] = total
+        top, rest = halves(u1)
+        ones = jnp.where(e_at == -2 * k, 1.0, 0.0).astype(BF16)
+        sums = dot_nn(jnp.concatenate([top, rest, (xf * both).astype(BF16)], axis=1), ones)
+        lsum = jnp.sum(lterm, axis=0, keepdims=True)
         both_states = st.astype(F32) * ds.astype(F32) * carry_rows(carry_own, k)
-        cs[k, 0:1, :] = jnp.sum(both_states[0:half], axis=0, keepdims=True)
-        cs[k, 1:2, :] = jnp.sum(both_states[half:], axis=0, keepdims=True)
-
-    pl.loop(0, pairs)(finish)
+        for j in range(2):
+            mine = low[0:1] if j == 0 else jnp.logical_not(low[0:1])
+            cs[k, j : j + 1, :] = jnp.where(mine, lsum, 0.0) + jnp.sum(
+                both_states[j * half : (j + 1) * half], axis=0, keepdims=True
+            )
+        return sums
+
+    @pl.loop(0, pairs // 2)
+    def _(k):
+        rr[...] += finish(2 * k) + finish(2 * k + 1)
 
     x_rim = remote(gp.at[pl.ds(0, 8)], nxt_x, nx_send, nx_recv, before)
 
     @pl.when(has_prev)
     def _():
         x_rim.start()
-
-    tri = jnp.where(r_id >= c_id, 1.0, 0.0)
-    dt_sig = sigmoid(dt)
-    pos2 = lax.broadcasted_iota(jnp.int32, (2, rows), 1) == rows - 1
-    cums, direct = [], []
-    for k in range(pairs):
-        extra = jnp.sum(rr[k, 4:6, :], axis=1, keepdims=True) + jnp.sum(cs[k, 0:2, :], axis=1, keepdims=True)
-        cums.append(rr[k, 0:2, :] + jnp.where(pos2, extra, 0.0))
-        direct.append(rr[k, 2:4, :])
-    d_log = exact_nn(jnp.concatenate(cums, axis=0), tri)
-    gdt_ref[...] = (jnp.concatenate(direct, axis=0) - decay * d_log) * dt_sig
-
-    @pl.when(has_next)
-    def _():
-        x_rim.wait_recv()
-
-    gp[rows:, :] = nxt_x[...]
-
-    @pl.loop(0, pairs)
-    def _(k):
-        cols = pl.ds(pl.multiple_of(k * LANES, LANES), LANES)
-        weight = wx_ref[:, cols].astype(F32)
-        total = weight[taps - 1 : taps] * gp[0:rows, cols]
-        for off in range(1, taps):
-            total = total + weight[taps - 1 - off : taps - off] * gp[off : off + rows, cols]
-        gx_ref[:, cols] = total.astype(BF16)
 
     for off in range(1, n_head):
         source = lax.rem(head + n_head - off, n_head)
@@ -435,6 +429,28 @@
     def _():
         bc_rim.start()
 
+    tri = jnp.where(r_id >= c_id, 1.0, 0.0)
+    turned_sums = jnp.transpose(rr[...])
+    extra = jnp.concatenate([cs[k, 0:2, :] for k in range(pairs)], axis=0)
+    extra = jnp.sum(extra, axis=1, keepdims=True)
+    d_log = exact_nn(turned_sums[:heads] + jnp.where(pos == rows - 1, extra, 0.0), tri)
+    gdt_ref[...] = (turned_sums[heads : 2 * heads] - decay * d_log) * sigmoid(dt)
+
+    @pl.when(has_next)
+    def _():
+        x_rim.wait_recv()
+
+    gp[rows:, :] = nxt_x[...]
+
+    @pl.loop(0, pairs)
+    def _(k):
+        cols = pl.ds(pl.multiple_of(k * LANES, LANES), LANES)
+        weight = wx_ref[:, cols].astype(F32)
+        total = weight[taps - 1 : taps] * gp[0:rows, cols]
+        for off in range(1, taps):
+            total = total + weight[taps - 1 - off : taps - off] * gp[off : off + rows, cols]
+        gx_ref[:, cols] = total.astype(BF16)
+
     for copy in sends:
         copy.wait_send()
 
@@ -472,6 +488,26 @@
     def _():
         x_rim.wait_send()
         bc_rim.wait_send()
+
+
+def hand_over(*refs):
+    count = (len(refs) - 1) // 2
+    sems = refs[-1]
+    copies = []
+    for at in range(count):
+        source, target = refs[at], refs[count + at]
+        total = source.shape[0]
+        pieces = PIECES if total % (PIECES * RIM) == 0 else 1
+        size = total // pieces
+        for piece in range(pieces):
+            rows = pl.ds(piece * size, size)
+            copies.append(
+                pltpu.make_async_copy(source.at[rows], target.at[rows], sems.at[len(copies)])
+            )
+    for copy in copies:
+        copy.start()
+    for copy in copies:
+        copy.wait()
 
 
 def body(n_ctx, n_head, x_raw, bc_raw, conv_x_w, conv_bc_w, dt_raw, a_log, d_skip, doc_starts, grad_y):
@@ -489,7 +525,7 @@
     scratch = [
         pltpu.VMEM((RIM, channels), BF16),
         pltpu.VMEM((RIM, 2 * nstate), BF16),
-        pltpu.VMEM((rows + 8, LANES), F32),
+        pltpu.VMEM((2, rows + 8, LANES), F32),
         pltpu.VMEM((rows + 8, 2 * nstate), F32),
         pltpu.VMEM((pairs, 8, rows), F32),
         state, state,
@@ -508,7 +544,7 @@
         pltpu.VMEM((rows, rows), F32),
         pltpu.VMEM((rows, nstate), F32),
         pltpu.VMEM((rows, nstate), F32),
-        pltpu.VMEM((pairs, 8, rows), F32),
+        pltpu.VMEM((rows, LANES), F32),
         pltpu.VMEM((pairs, 8, LANES), F32),
         pltpu.VMEM((n_head, rows, 2 * nstate), BF16),
         pltpu.VMEM((8, channels), F32),
@@ -520,14 +556,15 @@
         dma((n_head - 1,)), dma((n_head - 1,)),
         dma, dma, dma, dma,
     ]
-    return pl.pallas_call(
+    shapes = (
+        jax.ShapeDtypeStruct((rows, channels), BF16),
+        jax.ShapeDtypeStruct((rows, channels), BF16),
+        jax.ShapeDtypeStruct((rows, 2 * nstate), BF16),
+        jax.ShapeDtypeStruct((heads, rows), F32),
+    )
+    results = pl.pallas_call(
         functools.partial(kernel, n_ctx, n_head, pairs),
-        out_shape=(
-            jax.ShapeDtypeStruct((rows, channels), BF16),
-            jax.ShapeDtypeStruct((rows, channels), BF16),
-            jax.ShapeDtypeStruct((rows, 2 * nstate), BF16),
-            jax.ShapeDtypeStruct((heads, rows), F32),
-        ),
+        out_shape=shapes,
         in_specs=[vmem] * 5 + [smem, smem, smem, vmem],
         out_specs=(vmem, vmem, vmem, vmem),
         scratch_shapes=scratch,
@@ -538,6 +575,14 @@
     )(
         x_raw, bc_raw, conv_x_w, conv_bc_w, dt_raw, a_log, d_skip, doc_starts, grad_y
     )
+    anywhere = pl.BlockSpec(memory_space=pl.ANY)
+    return pl.pallas_call(
+        hand_over,
+        out_shape=shapes,
+        in_specs=[pl.BlockSpec(memory_space=pltpu.HBM)] * 4,
+        out_specs=(anywhere,) * 4,
+        scratch_shapes=[dma((4 * PIECES,))],
+    )(*results)
 
 
 def solution(mesh):

time: 70.3 us -> 130 us (1.85)
  Pallas kernels: 63.6 us -> 128 us
  local copies, waits for them, and re-layouts: 4.79 us -> 0 us
    pallas_call x0 -> x1, Pallas kernels: none -> 69.7 us  [body(): pl.pallas_call(hand_over, out_shape=shapes, in_specs=[pl.BlockSpec(memory...]
    pallas_call x1, Pallas kernels: 63.6 us -> 58.4 us  [body(): pl.pallas_call(functools.partial(kernel, n_ctx, n_head, pairs), out_shape...]
    unnamed x10 -> x0, local copies, waits for them, and re-layouts: 4.79 us -> none
where the time goes in v3:
time: 130 us; the launch traced here: 129 us
  Pallas kernels  128 us (98%)
    pallas_call x1, Pallas kernels, body(): pl.pallas_call(hand_over, out_shape=shapes, in_specs=[pl.BlockSpec(memory...  69.7 us
    pallas_call x1, Pallas kernels, body(): pl.pallas_call(functools.partial(kernel, n_ctx, n_head, pairs), out_shape...  58.4 us

profile of v3, /device:TPU:0, one launch (start us, length us, event | category | flops | bytes accessed | tf_op | source)
XLA Modules:
  0.0 129.4 jit_solution(1584908122951193944)
XLA Ops:
  1.3 58.4 %shard_map.120 = (bf16[256,2048]{1,0:T(8,128)(2,1)}, bf16[256,2048]{1,0:T(8,128)(2,1)}, bf16[256,256]{1,0:T(8,128)(2,1)}, f32[32,256]{1,0:T(8,128)}) custom-call(bf16[256,2048]{1,0:T(8,128)(2,1)} %x_ref.1, bf16[256,256]{1,0:T(8,128)(2,1)} %bc_ref.1, bf16[4,2048]{1,0:T(4,128)(2,1)} %wx_ref.1, bf16[4,256]{1,0:T(4,128)(2,1)} %wbc_ref.1, f32[32,256]{1,0:T(8,128)} %dt_ref.1, ...), custom_call_target="tpu_custom_call" | custom-call | flops 3000000000 | bytes 6291456 | tf_op jit(solution)/shard_map/pallas_call | solution.py:565
  59.7 69.7 %shard_map.121 = (bf16[256,2048]{1,0:T(8,128)(2,1)}, bf16[256,2048]{1,0:T(8,128)(2,1)}, bf16[256,256]{1,0:T(8,128)(2,1)}, f32[32,256]{1,0:T(8,128)}) custom-call(bf16[256,2048]{1,0:T(8,128)(2,1)} %get-tuple-element.8.refs_0_, bf16[256,2048]{1,0:T(8,128)(2,1)} %get-tuple-element.9.refs_1_, bf16[256,256]{1,0:T(8,128)(2,1)} %get-tuple-element.10.refs_2_, ...), custom_call_target="tpu_custom_call" | custom-call | tf_op jit(solution)/shard_map/pallas_call | solution.py:579

commit v4 on v3

--- a/solution.py
+++ b/solution.py
@@ -11,7 +11,7 @@
 BF16 = jnp.bfloat16
 LANES = 128
 RIM = 16
-LAG = 2
+LAG = 3
 PIECES = 4
 
 
@@ -325,8 +325,10 @@
 
     @pl.loop(0, pairs // 2)
     def _(k):
-        prepare(2 * k, 0)
-        prepare(2 * k + 1, 1)
+        late = k // (pairs // 4)
+        at = 4 * (k % (pairs // 4)) + jnp.where(late == 0, 1 - side, side)
+        prepare(at, 0)
+        prepare(at + 2, 1)
 
     carry_copy.wait_recv()
 
@@ -491,23 +493,9 @@
 
 
 def hand_over(*refs):
-    count = (len(refs) - 1) // 2
-    sems = refs[-1]
-    copies = []
+    count = len(refs) // 2
     for at in range(count):
-        source, target = refs[at], refs[count + at]
-        total = source.shape[0]
-        pieces = PIECES if total % (PIECES * RIM) == 0 else 1
-        size = total // pieces
-        for piece in range(pieces):
-            rows = pl.ds(piece * size, size)
-            copies.append(
-                pltpu.make_async_copy(source.at[rows], target.at[rows], sems.at[len(copies)])
-            )
-    for copy in copies:
-        copy.start()
-    for copy in copies:
-        copy.wait()
+        refs[count + at][...] = refs[at][...]
 
 
 def body(n_ctx, n_head, x_raw, bc_raw, conv_x_w, conv_bc_w, dt_raw, a_log, d_skip, doc_starts, grad_y):
@@ -575,13 +563,14 @@
     )(
         x_raw, bc_raw, conv_x_w, conv_bc_w, dt_raw, a_log, d_skip, doc_starts, grad_y
     )
-    anywhere = pl.BlockSpec(memory_space=pl.ANY)
+    blocks = [
+        pl.BlockSpec((rows // PIECES, channels), lambda i: (i, 0)),
+        pl.BlockSpec((rows // PIECES, channels), lambda i: (i, 0)),
+        pl.BlockSpec((rows // PIECES, 2 * nstate), lambda i: (i, 0)),
+        pl.BlockSpec((heads, rows), lambda i: (0, 0)),
+    ]
     return pl.pallas_call(
-        hand_over,
-        out_shape=shapes,
-        in_specs=[pl.BlockSpec(memory_space=pltpu.HBM)] * 4,
-        out_specs=(anywhere,) * 4,
-        scratch_shapes=[dma((4 * PIECES,))],
+        hand_over, grid=(PIECES,), out_shape=shapes, in_specs=blocks, out_specs=tuple(blocks)
     )(*results)
 
 

time: 130 us -> 60.6 us (0.47)
  Pallas kernels: 128 us -> 59.1 us
    pallas_call x1, Pallas kernels: 69.7 us -> 3.84 us  [body(): pl.pallas_call(hand_over, grid=(PIECES,), out_shape=shapes, in_specs=bloc...]
    pallas_call x1, Pallas kernels: 58.4 us -> 55.2 us  [body(): pl.pallas_call(functools.partial(kernel, n_ctx, n_head, pairs), out_shape...]
where the time goes in v4:
time: 60.6 us; the launch traced here: 60.4 us
  Pallas kernels  59.1 us (98%)
  between operations  1.29 us (2%)
    pallas_call x1, Pallas kernels, body(): pl.pallas_call(functools.partial(kernel, n_ctx, n_head, pairs), out_shape...  55.2 us
    pallas_call x1, Pallas kernels, body(): pl.pallas_call(hand_over, grid=(PIECES,), out_shape=shapes, in_specs=bloc...  3.84 us

profile of v4, /device:TPU:0, one launch (start us, length us, event | category | flops | bytes accessed | tf_op | source)
XLA Modules:
  0.0 60.4 jit_solution(2239163592807986055)
XLA Ops:
  1.3 55.2 %shard_map.120 = (bf16[256,2048]{1,0:T(8,128)(2,1)}, bf16[256,2048]{1,0:T(8,128)(2,1)}, bf16[256,256]{1,0:T(8,128)(2,1)}, f32[32,256]{1,0:T(8,128)}) custom-call(bf16[256,2048]{1,0:T(8,128)(2,1)} %x_ref.1, bf16[256,256]{1,0:T(8,128)(2,1)} %bc_ref.1, bf16[4,2048]{1,0:T(4,128)(2,1)} %wx_ref.1, bf16[4,256]{1,0:T(4,128)(2,1)} %wbc_ref.1, f32[32,256]{1,0:T(8,128)} %dt_ref.1, ...), custom_call_target="tpu_custom_call" | custom-call | flops 3000000000 | bytes 6291456 | tf_op jit(solution)/shard_map/pallas_call | solution.py:553
  56.5 3.8 %shard_map.121 = (bf16[256,2048]{1,0:T(8,128)(2,1)}, bf16[256,2048]{1,0:T(8,128)(2,1)}, bf16[256,256]{1,0:T(8,128)(2,1)}, f32[32,256]{1,0:T(8,128)}) custom-call(bf16[256,2048]{1,0:T(8,128)(2,1)} %get-tuple-element.8.refs_0_, bf16[256,2048]{1,0:T(8,128)(2,1)} %get-tuple-element.9.refs_1_, bf16[256,256]{1,0:T(8,128)(2,1)} %get-tuple-element.10.refs_2_, ...), custom_call_target="tpu_custom_call" | custom-call | tf_op jit(solution)/shard_map/pallas_call | solution.py:572

commit v5 on v4

--- a/solution.py
+++ b/solution.py
@@ -49,10 +49,10 @@
     halo_x, halo_bc, xp, bcp, stat, s_ref, g_ref, carry_own, carry_oth,
     s_out, s_in, g_out, g_in, fin, fout, bin_, bout, z_in, z_out, r_in, r_out,
     xc, sx, lx, edy, sgrad, intra, dsc, step_l, leave_l, enter_l, gp, gbp, sgrad_bc,
-    b_mat, c_mat, gram, bias, dgram, gb_acc, gc_acc, rr, cs, parts, nxt_x, nxt_bc,
+    b_mat, c_mat, gram, bias, dgram, gb_acc, gc_acc, rr, cs, parts, whole_part, summed, nxt_x, nxt_bc,
     hx_send, hx_recv, hb_send, hb_recv, f_send, f_recv, b_send, b_recv, c_send, c_recv,
     s_send, s_recv, g_send, g_recv, z_send, z_recv, r_send, r_recv,
-    p_send, p_recv, nx_send, nx_recv, nb_send, nb_recv,
+    p_send, p_recv, q_send, q_recv, nx_send, nx_recv, nb_send, nb_recv,
 ):
     rows = x_ref.shape[0]
     heads = dt_ref.shape[0]
@@ -323,18 +323,24 @@
             intra[rows_h, cols] = jnp.where(low[:mid], outs[h], outs[2 + h])
             dsc[rows_h, cols] = jnp.where(low[:mid], backs[0][h], backs[1][h])
 
-    @pl.loop(0, pairs // 2)
+    @pl.loop(0, pairs // 4)
     def _(k):
-        late = k // (pairs // 4)
-        at = 4 * (k % (pairs // 4)) + jnp.where(late == 0, 1 - side, side)
-        prepare(at, 0)
-        prepare(at + 2, 1)
+        prepare(4 * k + 1 - side, 0)
+        prepare(4 * k + 3 - side, 1)
 
     carry_copy.wait_recv()
 
-    @pl.loop(0, max(pairs, own_count + LAG * (duos - 1)))
+    @pl.loop(0, pairs // 4)
+    def _(k):
+        prepare(4 * k + side, 0)
+        prepare(4 * k + 2 + side, 1)
+        chain(k)
+
+    begun = pairs // 4
+
+    @pl.loop(0, max(pairs, own_count + LAG * (duos - 1) - begun))
     def _(i):
-        chain(i)
+        chain(i + begun)
 
         @pl.when(i < pairs)
         def _():
@@ -362,14 +368,33 @@
     top, rest = halves(dgram[...])
     grad_c = gc_acc[...] + dot_nn(top, b_mat[...]) + dot_nn(rest, b_mat[...])
     grad_b = gb_acc[...] + dot_tn(top, c_mat[...]) + dot_tn(rest, c_mat[...])
-    parts[head, :, 0:nstate] = grad_b.astype(BF16)
-    parts[head, :, nstate:] = grad_c.astype(BF16)
-    sends = []
+    share = rows // n_head
+    whole_part[:, 0:nstate] = grad_b.astype(BF16)
+    whole_part[:, nstate:] = grad_c.astype(BF16)
+
+    def rows_of(place):
+        return pl.ds(pl.multiple_of(place * share, share), share)
+
+    def peer(off):
+        return lax.rem(head + off, n_head)
+
+    scatters, gathers = [], []
     for off in range(1, n_head):
-        to = (ctx, lax.rem(head + off, n_head))
-        copy = remote(parts.at[head], parts.at[head], p_send.at[off - 1], p_recv.at[off - 1], to)
+        scatters.append(
+            remote(
+                whole_part.at[rows_of(peer(off))], parts.at[head],
+                p_send.at[off - 1], p_recv.at[off - 1], (ctx, peer(off)),
+            )
+        )
+        gathers.append(
+            remote(
+                summed.at[rows_of(head)], summed.at[rows_of(head)],
+                q_send.at[off - 1], q_recv.at[off - 1], (ctx, peer(off)),
+            )
+        )
+    for copy in scatters:
         copy.start()
-        sends.append(copy)
+    parts[head] = whole_part[rows_of(head), :]
 
     e_row = lax.broadcasted_iota(jnp.int32, (3 * LANES, LANES), 0)
     e_col = lax.broadcasted_iota(jnp.int32, (3 * LANES, LANES), 1)
@@ -405,26 +430,32 @@
             )
         return sums
 
-    @pl.loop(0, pairs // 2)
+    @pl.loop(0, pairs // 4)
     def _(k):
         rr[...] += finish(2 * k) + finish(2 * k + 1)
 
-    x_rim = remote(gp.at[pl.ds(0, 8)], nxt_x, nx_send, nx_recv, before)
-
-    @pl.when(has_prev)
-    def _():
-        x_rim.start()
-
-    for off in range(1, n_head):
-        source = lax.rem(head + n_head - off, n_head)
-        remote(
-            parts.at[source], parts.at[source], p_send.at[off - 1], p_recv.at[off - 1],
-            (ctx, lax.rem(head + off, n_head)),
-        ).wait_recv()
+    for copy in scatters:
+        copy.wait_recv()
     total = parts[0].astype(F32)
     for other in range(1, n_head):
         total = total + parts[other].astype(F32)
-    gbp[0:rows, :] = total * sgrad_bc[...]
+    summed[rows_of(head), :] = total.astype(BF16)
+    for copy in gathers:
+        copy.start()
+
+    @pl.loop(pairs // 4, pairs // 2)
+    def _(k):
+        rr[...] += finish(2 * k) + finish(2 * k + 1)
+
+    x_rim = remote(gp.at[pl.ds(0, 8)], nxt_x, nx_send, nx_recv, before)
+
+    @pl.when(has_prev)
+    def _():
+        x_rim.start()
+
+    for copy in gathers:
+        copy.wait_recv()
+    gbp[0:rows, :] = summed[...].astype(F32) * sgrad_bc[...]
     bc_rim = remote(gbp.at[pl.ds(0, 8)], nxt_bc, nb_send, nb_recv, before)
 
     @pl.when(has_prev)
@@ -453,7 +484,7 @@
             total = total + weight[taps - 1 - off : taps - off] * gp[off : off + rows, cols]
         gx_ref[:, cols] = total.astype(BF16)
 
-    for copy in sends:
+    for copy in scatters + gathers:
         copy.wait_send()
 
     carry_copy.wait_send()
@@ -534,14 +565,16 @@
         pltpu.VMEM((rows, nstate), F32),
         pltpu.VMEM((rows, LANES), F32),
         pltpu.VMEM((pairs, 8, LANES), F32),
-        pltpu.VMEM((n_head, rows, 2 * nstate), BF16),
+        pltpu.VMEM((n_head, rows // n_head, 2 * nstate), BF16),
+        pltpu.VMEM((rows, 2 * nstate), BF16),
+        pltpu.VMEM((rows, 2 * nstate), BF16),
         pltpu.VMEM((8, channels), F32),
         pltpu.VMEM((8, 2 * nstate), F32),
         dma, dma, dma, dma,
         dma((pairs,)), dma((pairs,)), dma((pairs,)), dma((pairs,)), dma, dma,
         dma((pairs,)), dma((pairs,)), dma((pairs,)), dma((pairs,)),
         dma((pairs,)), dma((pairs,)), dma((pairs,)), dma((pairs,)),
-        dma((n_head - 1,)), dma((n_head - 1,)),
+        dma((n_head - 1,)), dma((n_head - 1,)), dma((n_head - 1,)), dma((n_head - 1,)),
         dma, dma, dma, dma,
     ]
     shapes = (

time: 60.6 us -> 59.9 us (0.988)
  Pallas kernels: 59.1 us -> 58.4 us
    pallas_call x1, Pallas kernels: 55.2 us -> 54.6 us  [body(): pl.pallas_call(functools.partial(kernel, n_ctx, n_head, pairs), out_shape...]
where the time goes in v5:
time: 59.9 us; the launch traced here: 59.7 us
  Pallas kernels  58.4 us (97%)
  between operations  1.29 us (2%)
    pallas_call x1, Pallas kernels, body(): pl.pallas_call(functools.partial(kernel, n_ctx, n_head, pairs), out_shape...  54.6 us
    pallas_call x1, Pallas kernels, body(): pl.pallas_call(hand_over, grid=(PIECES,), out_shape=shapes, in_specs=bloc...  3.84 us

profile of v5, /device:TPU:0, one launch (start us, length us, event | category | flops | bytes accessed | tf_op | source)
XLA Modules:
  0.0 59.7 jit_solution(3918938865315221265)
XLA Ops:
  1.3 54.6 %shard_map.120 = (bf16[256,2048]{1,0:T(8,128)(2,1)}, bf16[256,2048]{1,0:T(8,128)(2,1)}, bf16[256,256]{1,0:T(8,128)(2,1)}, f32[32,256]{1,0:T(8,128)}) custom-call(bf16[256,2048]{1,0:T(8,128)(2,1)} %x_ref.1, bf16[256,256]{1,0:T(8,128)(2,1)} %bc_ref.1, bf16[4,2048]{1,0:T(4,128)(2,1)} %wx_ref.1, bf16[4,256]{1,0:T(4,128)(2,1)} %wbc_ref.1, f32[32,256]{1,0:T(8,128)} %dt_ref.1, ...), custom_call_target="tpu_custom_call" | custom-call | flops 3000000000 | bytes 6291456 | tf_op jit(solution)/shard_map/pallas_call | solution.py:586
  55.9 3.8 %shard_map.121 = (bf16[256,2048]{1,0:T(8,128)(2,1)}, bf16[256,2048]{1,0:T(8,128)(2,1)}, bf16[256,256]{1,0:T(8,128)(2,1)}, f32[32,256]{1,0:T(8,128)}) custom-call(bf16[256,2048]{1,0:T(8,128)(2,1)} %get-tuple-element.8.refs_0_, bf16[256,2048]{1,0:T(8,128)(2,1)} %get-tuple-element.9.refs_1_, bf16[256,256]{1,0:T(8,128)(2,1)} %get-tuple-element.10.refs_2_, ...), custom_call_target="tpu_custom_call" | custom-call | tf_op jit(solution)/shard_map/pallas_call | solution.py:605
